TPU v7x, 32 devices: a whole 2x2x4 slice. The times are simulated.
32 devices in a mesh: gx: 2 (over y), gz: 4 (over x, core), gy: 4 (over z).
Axes of the slice: x: 2, y: 2, z: 4, core: 2. Of those that a mesh axis runs over, the one named last changes fastest.
Arguments:
- gas_field: float32 [3, 32, 64, 512], P(None, 'gx', 'gy', 'gz'), may hold values from -6 to 6
- velocity: float32 [2048, 3, 128], P(('gx', 'gz', 'gy')), may hold values from -6 to 6
- fraction: float32 [2048, 3, 128], P(('gx', 'gz', 'gy')), may hold values from 0 to 1
- response: float32 [2048, 128], P(('gx', 'gz', 'gy')), may hold values from 0.25 to 2
- cell_index: int32 [2048, 128], P(('gx', 'gz', 'gy')), may hold values from 0 to 127
- brick_index: int32 [2048], P(('gx', 'gz', 'gy')), may hold values from 0 to 255
- crossing: int32 [192, 8], P(('gx', 'gz', 'gy')), may hold values from -1 to 63, as said below
Outputs:
- gas_next: float32 [3, 32, 64, 512], P(None, 'gx', 'gy', 'gz')
- velocity_next: float32 [2048, 3, 128], P(('gx', 'gz', 'gy'))
- arrivals: float32 [192, 8, 7, 128], P(('gx', 'gz', 'gy'))
Inputs may be any that keep to these rules, and one draw needn't show every extreme that they name: `crossing`: row 6 d + f lists the blocks of tile d (numbers 0 to 63 within the tile) that leave through face f (+x, -x, +y, -y, +z, -z): listed blocks first, then -1. No block is listed twice in one tile. Some face of some tile lists 8 blocks.
All inputs are finite; a program needn't handle non-finite values.
Results may differ from a plain program's by a relative error of at most 0.0003.
Values sent between devices are 32-bit elements; how exact they have to be, the bound alone decides.
No kernel may reach another device: no remote copies, remote signals or barrier semaphores. Data moves between devices by JAX's collectives and lax.ppermute only.
A program may use at most 128 MiB of HBM per device.

v0:
```python
import functools

import jax
import jax.numpy as jnp
from jax import lax
from jax.experimental import pallas as pl
from jax.experimental.pallas import tpu as pltpu
from jax.sharding import PartitionSpec as P

BX = 4
BY = 4
BZ = 8

TIME_STEP = 0.25
VISCOSITY = 0.4

LANES = 128
PACK = 32
HEAD = 8
ROWS_Y = 24
UNROLL = 4

VMEM = pl.BlockSpec(memory_space=pltpu.VMEM)
SMEM = pl.BlockSpec(memory_space=pltpu.SMEM)


def moved_along(block, axis, distance):
    count = lax.axis_size(axis)
    return lax.ppermute(block, axis, [(i, (i + distance) % count) for i in range(count)])


def call(body, outs, *operands, smem=(), scratch=(), aliases=None, cost=None):
    return pl.pallas_call(
        body,
        out_shape=[jax.ShapeDtypeStruct(shape, jnp.float32) for shape in outs],
        in_specs=[SMEM if i in smem else VMEM for i in range(len(operands))],
        out_specs=[VMEM] * len(outs),
        scratch_shapes=list(scratch),
        input_output_aliases=aliases or {},
        compiler_params=pltpu.CompilerParams(vmem_limit_bytes=40 * 1024 * 1024),
        cost_estimate=cost,
    )(*operands)


def lane_ids(rows):
    return lax.broadcasted_iota(jnp.int32, (rows, LANES), 1)


def turned(value, shift):
    shift = shift % LANES
    return pltpu.roll(value, shift, 1) if shift else value


def pack_face_kernel(gas_ref, face_ref):
    comps, size_x, size_y, _ = gas_ref.shape
    lane = lane_ids(size_y)
    face = jnp.zeros((size_y, LANES), jnp.float32)
    for c in range(comps):
        for x in range(size_x):
            place = PACK * c + x
            face = jnp.where(lane == place, turned(gas_ref[c, x], place), face)
    face_ref[...] = face


def halo_y_kernel(gas_ref, face_ref, from_x_ref, out_ref):
    comps, size_x, size_y, _ = gas_ref.shape
    for c in range(comps):
        out_ref[c * size_x : (c + 1) * size_x] = gas_ref[c, :, 0]
        out_ref[comps * size_x + c : comps * size_x + c + 1] = from_x_ref[c * size_y : c * size_y + 1]
    start = comps * size_y
    own = face_ref[0:8]
    far = turned(from_x_ref[start : start + 8], size_x)
    line = jnp.where(lane_ids(8) % PACK == size_x, far, own)
    out_ref[comps * size_x + comps : comps * size_x + comps + 1] = line[0:1]


def step_kernel(
    loading, brick_ref, crossing_ref, gas_ref, face_ref, from_x_ref, from_y_ref,
    velocity_ref, fraction_ref, response_ref, cell_ref,
    moved_ref, base_ref, to_y_ref, to_x_ref, to_z_ref, out_ref,
    grid_ref, deposit_ref, weight_ref, rows_ref,
):
    comps, size_x, size_y, size_z = gas_ref.shape
    nblocks = velocity_ref.shape[1]
    count_y, count_z = size_y // BY, size_z // BZ
    reach_x, reach_y = BX + 1, 8
    inside = lax.axis_index("gy") != lax.axis_size("gy") - 1
    lane = lane_ids(8)
    sub = lax.broadcasted_iota(jnp.int32, (8, LANES), 0)
    first_lane = lane == 0

    def row_of(sel, c, x):
        return HEAD + ((sel * comps + c) * (size_x + 1) + x) * ROWS_Y

    grid_ref[0:HEAD] = jnp.zeros((HEAD, LANES), jnp.float32)
    edge = comps * size_y
    for c in range(comps):
        for x in range(size_x + 1):
            if x < size_x:
                plane, line = gas_ref[c, x], from_y_ref[c * size_x + x : c * size_x + x + 1]
                far = turned(face_ref[...], -(PACK * c + x))
            else:
                plane = from_x_ref[c * size_y : (c + 1) * size_y]
                line = from_y_ref[comps * size_x + c : comps * size_x + c + 1]
                far = turned(from_x_ref[edge : edge + size_y], -PACK * c)
            corner = from_y_ref[comps * size_x + comps : comps * size_x + comps + 1]
            corner = turned(jnp.broadcast_to(corner, (8, LANES)), -(PACK * c + x))
            line = jnp.broadcast_to(line, (8, LANES))
            kept = (sub == 0) & inside
            zeros = jnp.zeros((8, LANES), jnp.float32)
            at = row_of(0, c, x)
            grid_ref[at : at + size_y] = plane
            grid_ref[at + size_y : at + ROWS_Y] = jnp.where(kept, line, zeros)
            at = row_of(1, c, x)
            grid_ref[at : at + size_y] = jnp.where(lane_ids(size_y) == 0, far, plane)
            grid_ref[at + size_y : at + ROWS_Y] = jnp.where(kept, jnp.where(first_lane, corner, line), zeros)
    deposit_ref[...] = jnp.zeros_like(deposit_ref)

    cells = cell_ref[...]
    cell_x, cell_y, cell_z = cells // (BY * BZ), cells // BZ % BY, cells % BZ
    along_x, along_z = fraction_ref[0], fraction_ref[2]
    for a in range(reach_x):
        weight_ref[a] = jnp.where(cell_x == a, 1.0 - along_x, 0.0) + jnp.where(cell_x == a - 1, along_x, 0.0)
    low, high = 1.0 - along_z, along_z
    low_main = low.astype(jnp.bfloat16).astype(jnp.float32)
    high_main = high.astype(jnp.bfloat16).astype(jnp.float32)
    rows_ref[0] = cell_y.astype(jnp.float32)
    rows_ref[1] = cell_z.astype(jnp.float32)
    rows_ref[2] = low_main
    rows_ref[3] = low - low_main
    rows_ref[4] = high_main
    rows_ref[5] = high - high_main
    rows_ref[6] = 1.0 / response_ref[...]

    packed_z = lax.broadcasted_iota(jnp.int32, (16, LANES), 0).astype(jnp.float32).astype(jnp.bfloat16)
    sub_y = sub.astype(jnp.float32)
    last = count_z - 1

    def one(k):
        brick = brick_ref[k]
        brick_x = brick // (count_y * count_z)
        brick_y = brick // count_z % count_y
        brick_z = brick % count_z
        sel = jnp.where(brick_z == last, 1, 0)
        start = HEAD + (sel * comps * (size_x + 1) + brick_x * BX) * ROWS_Y + brick_y * BY

        def row(i):
            return rows_ref[i, pl.ds(k, 1)]

        def tall(value):
            return jnp.broadcast_to(value, (16, LANES)).astype(jnp.bfloat16)

        place = row(1) + (brick_z * BZ).astype(jnp.float32)
        after = place + 1.0
        after = jnp.where(after == float(size_z), 0.0, after)
        place, after = tall(place), tall(after)
        low_main, low_rest, high_main, high_rest = [tall(row(i)) for i in (2, 3, 4, 5)]
        nothing = jnp.zeros((16, LANES), jnp.bfloat16)
        main, rest = [], []
        for j in range(size_z // 16):
            here = packed_z + jnp.bfloat16(16 * j)
            at_low, at_high = here == place, here == after
            main.append(jnp.where(at_low, low_main, jnp.where(at_high, high_main, nothing)))
            rest.append(jnp.where(at_low, low_rest, jnp.where(at_high, high_rest, nothing)))
        main, rest = jnp.concatenate(main, axis=0), jnp.concatenate(rest, axis=0)
        both = jnp.concatenate([main, rest], axis=1)
        table = jnp.concatenate([both, both], axis=0)
        both_t = jnp.concatenate([main, rest], axis=0)
        table_t = jnp.concatenate([both_t, both_t], axis=1)

        def cut(value):
            top = value.astype(jnp.bfloat16)
            return jnp.concatenate([top, (value - top.astype(jnp.float32)).astype(jnp.bfloat16)], axis=1)

        offsets = [(c * (size_x + 1) + a) * ROWS_Y for c in range(comps) for a in range(reach_x)]
        window = jnp.concatenate([grid_ref[pl.ds(start + o, reach_y)] for o in offsets], axis=0)
        lines = lax.dot_general(cut(window), table, (((1,), (0,)), ((), ())), preferred_element_type=jnp.float32)
        lines = lines[:, :LANES] + lines[:, LANES:]
        lines = lines.reshape(comps, reach_x, reach_y, LANES)
        weight_x = [weight_ref[a, pl.ds(k, 1)] for a in range(reach_x)]
        in_y, along_y = row(0), fraction_ref[1, pl.ds(k, 1)]
        weight_y = jnp.where(sub_y == in_y, 1.0 - along_y, 0.0) + jnp.where(sub_y == in_y + 1.0, along_y, 0.0)
        rate = row(6)
        pushed = []
        for c in range(comps):
            total = lines[c, 0] * weight_x[0]
            for a in range(1, reach_x):
                total = total + lines[c, a] * weight_x[a]
            gas_sample = jnp.sum(total * weight_y, axis=0, keepdims=True)
            moving = velocity_ref[c, pl.ds(k, 1)]
            drag = (gas_sample - moving) * rate
            moved_ref[c, pl.ds(k, 1)] = moving + TIME_STEP * drag
            spread = drag * weight_y
            pushed.extend(spread * weight_x[a] for a in range(reach_x))
        pushed = jnp.concatenate(pushed, axis=0)
        shares = lax.dot_general(cut(pushed), table_t, (((1,), (1,)), ((), ())), preferred_element_type=jnp.float32)
        shares = shares[:, :LANES] + shares[:, LANES:]
        return start, offsets, shares

    @pl.loop(0, nblocks // UNROLL)
    def _(group):
        results = [one(group * UNROLL + u) for u in range(UNROLL)]
        for start, offsets, shares in results:
            for i, o in enumerate(offsets):
                spot = pl.ds(start + o, reach_y)
                deposit_ref[spot] = deposit_ref[spot] + shares[i * reach_y : (i + 1) * reach_y]

    push, diffuse = -TIME_STEP * loading, TIME_STEP * VISCOSITY
    for y in range(0, size_y, 8):
        to_z_ref[y : y + 8] = jnp.zeros((8, LANES), jnp.float32)
    tall_lane = lane_ids(ROWS_Y)
    face_out = jnp.zeros((ROWS_Y, LANES), jnp.float32)
    for c in range(comps):
        for x in range(size_x + 1):
            at, up = row_of(0, c, x), row_of(1, c, x)
            wrapped = deposit_ref[up : up + ROWS_Y]
            total = push * (deposit_ref[at : at + ROWS_Y] + jnp.where(tall_lane == 0, 0.0, wrapped))
            beyond = push * wrapped
            if x < size_x:
                here = grid_ref[at : at + size_y]
                laplace = grid_ref[at + ROWS_Y : at + ROWS_Y + size_y]
                if x:
                    laplace = laplace + grid_ref[at - ROWS_Y : at - ROWS_Y + size_y]
                laplace = laplace + grid_ref[at + 1 : at + 1 + size_y] + grid_ref[at - 1 : at - 1 + size_y]
                behind = turned(here, 1)
                ahead = turned(grid_ref[up : up + size_y], -1)
                laplace = laplace + ahead + jnp.where(lane_ids(size_y) == 0, 0.0, behind) - 6.0 * here
                base_ref[c, x] = here + diffuse * laplace + total[:size_y]
                line = diffuse * here[size_y - 1 :] + total[size_y : size_y + 1]
                beyond = jnp.concatenate([beyond[:size_y] + diffuse * behind, beyond[size_y:]], axis=0)
            else:
                here = grid_ref[at - ROWS_Y : at - ROWS_Y + size_y]
                to_x_ref[c * size_y : (c + 1) * size_y] = diffuse * here + total[:size_y]
                line = total[size_y : size_y + 1]
            to_y_ref[c * ROWS_Y + x : c * ROWS_Y + x + 1] = line
            place = PACK * c + x
            face_out = jnp.where(tall_lane == place, turned(beyond, place), face_out)
    to_z_ref[...] = face_out[:size_y]
    to_y_ref[size_x + 1 : size_x + 2] = face_out[size_y : size_y + 1]

    capacity = crossing_ref.shape[1]
    for face in range(6):
        for slot in range(capacity):
            block = crossing_ref[face, slot]
            live = block >= 0
            spot = pl.ds(jnp.maximum(block, 0), 1)
            state = [moved_ref[c, spot] for c in range(comps)]
            state = state + [fraction_ref[c, spot] + TIME_STEP * state[c] for c in range(comps)]
            state.append(response_ref[spot])
            for i, value in enumerate(state):
                out_ref[face, i, slot : slot + 1] = jnp.where(live, value, 0.0)


def relay_x_kernel(size_x, size_y, comps, from_y_ref, to_x_ref, to_z_ref, x_ref, z_ref):
    inside = lax.axis_index("gy") != 0
    x_ref[...] = to_x_ref[...]
    z_ref[...] = to_z_ref[...]
    for c in range(comps):
        at = c * ROWS_Y + size_x
        spot = slice(c * size_y, c * size_y + 1)
        x_ref[spot] = to_x_ref[spot] + jnp.where(inside, from_y_ref[at : at + 1], 0.0)
    line = jnp.where(inside, from_y_ref[size_x + 1 : size_x + 2], 0.0)
    z_ref[0:1] = to_z_ref[0:1] + line
    edge = comps * size_y
    x_ref[edge : edge + size_y] = z_ref[...]


def relay_z_kernel(size_x, comps, edge, from_x_ref, to_z_ref, z_ref):
    size_y = to_z_ref.shape[0]
    lane = lane_ids(size_y)
    far = turned(from_x_ref[edge : edge + size_y], -size_x)
    z_ref[...] = to_z_ref[...] + jnp.where(lane % PACK == 0, far, 0.0)


def finish_kernel(base_ref, from_y_ref, from_x_ref, from_z_ref, gas_ref):
    comps, size_x, size_y, _ = base_ref.shape
    inside = lax.axis_index("gy") != 0
    lane = lane_ids(size_y)
    row = lax.broadcasted_iota(jnp.int32, (size_y, LANES), 0)
    first = (row == 0) & inside
    face = from_z_ref[...]
    for c in range(comps):
        for x in range(size_x):
            total = base_ref[c, x]
            line = jnp.broadcast_to(from_y_ref[c * ROWS_Y + x : c * ROWS_Y + x + 1], (size_y, LANES))
            total = total + jnp.where(first, line, 0.0)
            if x == 0:
                total = total + from_x_ref[c * size_y : (c + 1) * size_y]
            total = total + jnp.where(lane == 0, turned(face, -(PACK * c + x)), 0.0)
            gas_ref[c, x] = total


def per_device(gas_field, velocity, fraction, response, cell_index, brick_index, crossing):
    comps, size_x, size_y, size_z = gas_field.shape
    nblocks = velocity.shape[0]
    loading = 0.5 * size_x * size_y * size_z / (nblocks * 128)
    velocity = jnp.transpose(velocity, (1, 0, 2))
    fraction = jnp.transpose(fraction, (1, 0, 2))

    (face,) = call(pack_face_kernel, [(size_y, LANES)], gas_field)
    face = moved_along(face, "gz", -1)
    plane = jnp.concatenate([gas_field[:, 0].reshape(comps * size_y, LANES), face], axis=0)
    from_x = moved_along(plane, "gx", -1)
    rows = -(-(comps * size_x + comps + 1) // 8) * 8
    (lines,) = call(halo_y_kernel, [(rows, LANES)], gas_field, face, from_x)
    from_y = moved_along(lines, "gy", -1)

    grid_rows = HEAD + 2 * comps * (size_x + 1) * ROWS_Y
    moved, base, to_y, to_x, to_z, leaving = call(
        functools.partial(step_kernel, loading),
        [
            (comps, nblocks, LANES),
            (comps, size_x, size_y, LANES),
            (comps * ROWS_Y, LANES),
            (comps * size_y, LANES),
            (size_y, LANES),
            (6, 7, crossing.shape[1], LANES),
        ],
        brick_index, crossing, gas_field, face, from_x, from_y, velocity, fraction, response, cell_index,
        smem=(0, 1),
        scratch=(
            pltpu.VMEM((grid_rows, LANES), jnp.float32),
            pltpu.VMEM((grid_rows, LANES), jnp.float32),
            pltpu.VMEM((BX + 1, nblocks, LANES), jnp.float32),
            pltpu.VMEM((7, nblocks, LANES), jnp.float32),
        ),
    )

    def flat(array):
        return array.reshape(-1, LANES)

    def joined(*arrays):
        return jnp.concatenate([flat(array) for array in arrays], axis=0)

    count = flat(leaving[0]).shape[0]
    got_y = moved_along(joined(to_y, leaving[2]), "gy", 1)
    got_my = moved_along(leaving[3], "gy", -1)
    got_mz = moved_along(leaving[5], "gz", -1)
    edge = comps * size_y
    x_part, z_part = call(
        functools.partial(relay_x_kernel, size_x, size_y, comps),
        [(edge + size_y, LANES), (size_y, LANES)],
        got_y, jnp.concatenate([to_x, to_z], axis=0), to_z,
    )
    if lax.axis_size("gx") == 2:
        got_x = moved_along(joined(x_part, leaving[0], leaving[1]), "gx", 1)
        got_mx = got_x[edge + size_y + count :]
    else:
        got_x = moved_along(joined(x_part, leaving[0]), "gx", 1)
        got_mx = moved_along(leaving[1], "gx", -1)
    (z_part,) = call(functools.partial(relay_z_kernel, size_x, comps, edge), [(size_y, LANES)], got_x, z_part)
    got_z = moved_along(joined(z_part, leaving[4]), "gz", 1)
    (gas_next,) = call(finish_kernel, [gas_field.shape], base, got_y[: comps * ROWS_Y], got_x[:edge], got_z[:size_y])

    low = lax.axis_index("gy") == 0
    high = lax.axis_index("gy") == lax.axis_size("gy") - 1
    parts = [
        got_x[edge + size_y : edge + size_y + count],
        got_mx,
        jnp.where(low, 0.0, got_y[comps * ROWS_Y :]),
        jnp.where(high, 0.0, flat(got_my)),
        got_z[size_y:],
        got_mz,
    ]
    arrivals = jnp.stack([part.reshape(7, -1, LANES) for part in parts], axis=0)
    return gas_next, jnp.transpose(moved, (1, 0, 2)), jnp.transpose(arrivals, (0, 2, 1, 3))


def solution(mesh):
    owner = ("gx", "gz", "gy")
    in_specs = (
        P(None, "gx", "gy", "gz"),
        P(owner, None, None),
        P(owner, None, None),
        P(owner, None),
        P(owner, None),
        P(owner),
        P(owner, None),
    )
    out_specs = (
        P(None, "gx", "gy", "gz"),
        P(owner, None, None),
        P(owner, None, None, None),
    )
    return jax.shard_map(
        per_device, mesh=mesh, in_specs=in_specs, out_specs=out_specs, check_vma=False
    )
```

profile of v0, /device:TPU:0, one launch (start us, length us, event | category | flops | bytes accessed | tf_op | source)
XLA Modules:
  0.0 44.7 jit_solution(16741153275268290794)
XLA Ops:
  0.6 0.0 copy-start
  0.6 1.0 %copy-done = f32[3,16,16,128]{3,2,1,0:T(8,128)S(1)} copy-done((f32[3,16,16,128]{3,2,1,0:T(8,128)S(1)}, f32[3,16,16,128]{3,2,1,0:T(8,128)}, u32[]{:S(2)}) %copy-start) | copy-done | bytes 393240
  1.6 0.2 shard_map.94
  1.8 0.0 slice-start
  1.8 2.4 %collective-permute-start = (f32[16,128]{1,0:T(8,128)S(1)}, f32[16,128]{1,0:T(8,128)S(1)}, u32[]{:S(2)}, u32[]{:S(2)}) collective-permute-start(f32[16,128]{1,0:T(8,128)S(1)} %shard_map.94), channel_id=1, source_target_pairs={{0,12},{4,0},{8,4},{12,8},{1,13},{5,1},{9,5},{13,9},{2,14},{6,2},{... | collective-permute-start | bytes 24584 | tf_op jit(solution)/shard_map/ppermute | solution.py:29
  4.2 1.4 %collective-permute-done.face_ref = f32[16,128]{1,0:T(8,128)S(1)} collective-permute-done((f32[16,128]{1,0:T(8,128)S(1)}, f32[16,128]{1,0:T(8,128)S(1)}, u32[]{:S(2)}, u32[]{:S(2)}) %collective-permute-start) | collective-permute-done | bytes 8224 | tf_op jit(solution)/shard_map/ppermute | solution.py:29
  5.6 0.0 slice-done
  5.6 0.0 copy-start.1
  5.6 0.0 copy-start.2
  5.6 0.0 copy-start.3
  5.6 0.0 copy-start.4
  5.6 1.6 %collective-permute-start.1 = (f32[64,128]{1,0:T(8,128)S(1)}, f32[64,128]{1,0:T(8,128)S(1)}, u32[]{:S(2)}, u32[]{:S(2)}) collective-permute-start(f32[64,128]{1,0:T(8,128)S(1)} %pad_maximum_fusion.3), channel_id=1, source_target_pairs={{0,16},{16,0},{1,17},{17,1},{2,18},{18,2},{3,19},{19,3},{4,20},{20... | collective-permute-start | bytes 98312 | tf_op jit(solution)/shard_map/ppermute | solution.py:29
  7.2 2.4 %collective-permute-done.1.from_x_ref = f32[64,128]{1,0:T(8,128)S(1)} collective-permute-done((f32[64,128]{1,0:T(8,128)S(1)}, f32[64,128]{1,0:T(8,128)S(1)}, u32[]{:S(2)}, u32[]{:S(2)}) %collective-permute-start.1) | collective-permute-done | bytes 32800 | tf_op jit(solution)/shard_map/ppermute | solution.py:29
  9.7 0.0 copy-start.5
  9.7 0.1 shard_map.95
  9.7 3.6 %collective-permute-start.2 = (f32[56,128]{1,0:T(8,128)S(1)}, f32[56,128]{1,0:T(8,128)S(1)}, u32[]{:S(2)}, u32[]{:S(2)}) collective-permute-start(f32[56,128]{1,0:T(8,128)S(1)} %shard_map.95), channel_id=1, source_target_pairs={{0,3},{1,0},{2,1},{3,2},{4,7},{5,4},{6,5},{7,6},{8,11},{9,8},{10,9... | collective-permute-start | bytes 86024 | tf_op jit(solution)/shard_map/ppermute | solution.py:29
  13.3 1.6 %collective-permute-done.2.from_y_ref = f32[56,128]{1,0:T(8,128)S(1)} collective-permute-done((f32[56,128]{1,0:T(8,128)S(1)}, f32[56,128]{1,0:T(8,128)S(1)}, u32[]{:S(2)}, u32[]{:S(2)}) %collective-permute-start.2) | collective-permute-done | bytes 28704 | tf_op jit(solution)/shard_map/ppermute | solution.py:29
  14.9 0.0 copy-start.6
  14.9 0.0 copy-done.1
  14.9 0.0 copy-done.2
  14.9 0.0 copy-done.3
  14.9 0.0 copy-done.4
  14.9 0.0 copy-done.5
  14.9 0.6 %copy-done.6 = s32[64]{0:T(128)S(1)} copy-done((s32[64]{0:T(128)S(1)}, s32[64]{0:T(128)}, u32[]{:S(2)}) %copy-start.6) | copy-done | bytes 280
  15.6 13.0 %shard_map.96 = (f32[3,64,128]{2,1,0:T(8,128)}, f32[3,16,16,128]{3,2,1,0:T(8,128)S(1)}, f32[72,128]{1,0:T(8,128)S(1)}, f32[48,128]{1,0:T(8,128)S(1)}, f32[16,128...) custom-call(s32[64]{0:T(128)S(1)} %copy-done.6, s32[6,8]{1,0:T(8,128)S(1)} %copy-done.5, f32[3,16,16,128]{3,2,1,0:T(8,128)S(1)} %copy-done, ...), custom_call_target="tpu_custom_call" | custom-call | tf_op jit(solution)/shard_map/pallas_call | solution.py:33
  28.6 0.3 collective-permute-start.3
  29.0 6.0 %collective-permute-done.3.from_y_ref = f32[128,128]{1,0:T(8,128)S(1)} collective-permute-done((f32[128,128]{1,0:T(8,128)S(1)}, f32[128,128]{1,0:T(8,128)S(1)}, u32[]{:S(2)}, u32[]{:S(2)}) %collective-permute-start.3) | collective-permute-done | bytes 65568 | tf_op jit(solution)/shard_map/ppermute | solution.py:29
  35.0 1.7 %collective-permute-start.4 = (f32[176,128]{1,0:T(8,128)S(1)}, f32[176,128]{1,0:T(8,128)S(1)}, u32[]{:S(2)}, u32[]{:S(2)}) collective-permute-start(f32[176,128]{1,0:T(8,128)S(1)} %pad_maximum_fusion), channel_id=1, source_target_pairs={{0,16},{16,0},{1,17},{17,1},{2,18},{18,2},{3,19},{19,3},{4,20},{20... | collective-permute-start | bytes 270344 | tf_op jit(solution)/shard_map/ppermute | solution.py:29
  36.7 1.9 %collective-permute-start.6 = (f32[7,8,128]{2,1,0:T(8,128)S(1)}, f32[7,8,128]{2,1,0:T(8,128)S(1)}, u32[]{:S(2)}, u32[]{:S(2)}) collective-permute-start(f32[7,8,128]{2,1,0:T(8,128)S(1)} %get-tuple-element.20), channel_id=1, source_target_pairs={{0,3},{1,0},{2,1},{3,2},{4,7},{5,4},{6,5},{7,6},{8,11},{9,8},{10,9... | collective-permute-start | bytes 86024 | tf_op jit(solution)/shard_map/ppermute | solution.py:29
  38.7 0.0 collective-permute-start.7
  38.7 1.0 %collective-permute-done.4.from_x_ref = f32[176,128]{1,0:T(8,128)S(1)} collective-permute-done((f32[176,128]{1,0:T(8,128)S(1)}, f32[176,128]{1,0:T(8,128)S(1)}, u32[]{:S(2)}, u32[]{:S(2)}) %collective-permute-start.4) | collective-permute-done | bytes 90144 | tf_op jit(solution)/shard_map/ppermute | solution.py:29
  39.6 0.1 shard_map.98
  39.7 0.0 collective-permute-start.5
  39.8 0.9 %collective-permute-done.6 = f32[7,8,128]{2,1,0:T(8,128)S(1)} collective-permute-done((f32[7,8,128]{2,1,0:T(8,128)S(1)}, f32[7,8,128]{2,1,0:T(8,128)S(1)}, u32[]{:S(2)}, u32[]{:S(2)}) %collective-permute-start.6) | collective-permute-done | bytes 28704 | tf_op jit(solution)/shard_map/ppermute | solution.py:29
  40.6 2.5 %collective-permute-done.5 = f32[72,128]{1,0:T(8,128)S(1)} collective-permute-done((f32[72,128]{1,0:T(8,128)S(1)}, f32[72,128]{1,0:T(8,128)S(1)}, u32[]{:S(2)}, u32[]{:S(2)}) %collective-permute-start.5) | collective-permute-done | bytes 36896 | tf_op jit(solution)/shard_map/ppermute | solution.py:29
  43.1 0.9 %shard_map.99 = f32[3,16,16,128]{3,2,1,0:T(8,128)} custom-call(f32[3,16,16,128]{3,2,1,0:T(8,128)S(1)} %get-tuple-element.11.base_ref, f32[72,128]{1,0:T(8,128)S(1)} %slice.56.from_y_ref, f32[48,128]{1,0:T(8,128)S(1)} %slice.57.from_x_ref, f32[16,128]{1,0:T(8,128)S(1)} %slice.58.from_z_ref), custom_call_target="tpu_custom_call" | custom-call | tf_op jit(solution)/shard_map/pallas_call | solution.py:33
  44.0 0.0 collective-permute-done.7
  44.0 0.0 copy-start.7
  44.0 0.7 %copy-done.7 = f32[6,7,8,128]{3,2,1,0:T(8,128)} copy-done((f32[6,7,8,128]{3,2,1,0:T(8,128)}, f32[6,7,8,128]{3,2,1,0:T(8,128)S(1)}, u32[]{:S(2)}) %copy-start.7) | copy-done | bytes 172056
  (16 shorter events, 0.1 us)
Async XLA Ops:
  0.6 1.0 %copy-start = (f32[3,16,16,128]{3,2,1,0:T(8,128)S(1)}, f32[3,16,16,128]{3,2,1,0:T(8,128)}, u32[]{:S(2)}) copy-start(f32[3,16,16,128]{3,2,1,0:T(8,128)} %gas_ref.5) | copy-start | bytes 1179652
  1.8 3.8 %slice-start = ((f32[3,16,16,128]{3,2,1,0:T(8,128)}), f32[3,1,16,128]{3,2,1,0:T(8,128)S(1)}, s32[]{:S(2)}) async-start(f32[3,16,16,128]{3,2,1,0:T(8,128)} %gas_ref.5), calls=%async_computation | async-start | bytes 49152 | tf_op jit(solution)/shard_map/slice | solution.py:302
  1.8 3.8 %collective-permute-start = (f32[16,128]{1,0:T(8,128)S(1)}, f32[16,128]{1,0:T(8,128)S(1)}, u32[]{:S(2)}, u32[]{:S(2)}) collective-permute-start(f32[16,128]{1,0:T(8,128)S(1)} %shard_map.94), channel_id=1, source_target_pairs={{0,12},{4,0},{8,4},{12,8},{1,13},{5,1},{9,5},{13,9},{2,14},{6,2},{... | collective-permute-start | bytes 24584 | tf_op jit(solution)/shard_map/ppermute | solution.py:29
  5.6 9.3 %copy-start.1 = (f32[64,3,128]{2,0,1:T(8,128)S(1)}, f32[64,3,128]{2,0,1:T(8,128)}, u32[]{:S(2)}) copy-start(f32[64,3,128]{2,0,1:T(8,128)} %param.8) | copy-start | bytes 294916
  5.6 9.3 %copy-start.2 = (f32[64,3,128]{2,0,1:T(8,128)S(1)}, f32[64,3,128]{2,0,1:T(8,128)}, u32[]{:S(2)}) copy-start(f32[64,3,128]{2,0,1:T(8,128)} %param.9) | copy-start | bytes 294916
  5.6 9.3 %copy-start.3 = (f32[64,128]{1,0:T(8,128)S(1)}, f32[64,128]{1,0:T(8,128)}, u32[]{:S(2)}) copy-start(f32[64,128]{1,0:T(8,128)} %response_ref.1) | copy-start | bytes 98308
  5.6 9.3 %copy-start.4 = (s32[64,128]{1,0:T(8,128)S(1)}, s32[64,128]{1,0:T(8,128)}, u32[]{:S(2)}) copy-start(s32[64,128]{1,0:T(8,128)} %cell_ref.1) | copy-start | bytes 98308
  5.6 4.0 %collective-permute-start.1 = (f32[64,128]{1,0:T(8,128)S(1)}, f32[64,128]{1,0:T(8,128)S(1)}, u32[]{:S(2)}, u32[]{:S(2)}) collective-permute-start(f32[64,128]{1,0:T(8,128)S(1)} %pad_maximum_fusion.3), channel_id=1, source_target_pairs={{0,16},{16,0},{1,17},{17,1},{2,18},{18,2},{3,19},{19,3},{4,20},{20... | collective-permute-start | bytes 98312 | tf_op jit(solution)/shard_map/ppermute | solution.py:29
  9.7 5.3 %copy-start.5 = (s32[6,8]{1,0:T(8,128)S(1)}, s32[6,8]{1,0:T(8,128)}, u32[]{:S(2)}) copy-start(s32[6,8]{1,0:T(8,128)} %crossing_ref.1) | copy-start | bytes 580
  9.7 5.2 %collective-permute-start.2 = (f32[56,128]{1,0:T(8,128)S(1)}, f32[56,128]{1,0:T(8,128)S(1)}, u32[]{:S(2)}, u32[]{:S(2)}) collective-permute-start(f32[56,128]{1,0:T(8,128)S(1)} %shard_map.95), channel_id=1, source_target_pairs={{0,3},{1,0},{2,1},{3,2},{4,7},{5,4},{6,5},{7,6},{8,11},{9,8},{10,9... | collective-permute-start | bytes 86024 | tf_op jit(solution)/shard_map/ppermute | solution.py:29
  14.9 0.7 %copy-start.6 = (s32[64]{0:T(128)S(1)}, s32[64]{0:T(128)}, u32[]{:S(2)}) copy-start(s32[64]{0:T(128)} %brick_ref.1) | copy-start | bytes 772
  28.6 6.4 %collective-permute-start.3 = (f32[128,128]{1,0:T(8,128)S(1)}, f32[128,128]{1,0:T(8,128)S(1)}, u32[]{:S(2)}, u32[]{:S(2)}) collective-permute-start(f32[128,128]{1,0:T(8,128)S(1)} %pad_maximum_fusion.1), channel_id=1, source_target_pairs={{0,1},{1,2},{2,3},{3,0},{4,5},{5,6},{6,7},{7,4},{8,9},{9,10},{10,1... | collective-permute-start | bytes 196616 | tf_op jit(solution)/shard_map/ppermute | solution.py:29
  35.0 4.6 %collective-permute-start.4 = (f32[176,128]{1,0:T(8,128)S(1)}, f32[176,128]{1,0:T(8,128)S(1)}, u32[]{:S(2)}, u32[]{:S(2)}) collective-permute-start(f32[176,128]{1,0:T(8,128)S(1)} %pad_maximum_fusion), channel_id=1, source_target_pairs={{0,16},{16,0},{1,17},{17,1},{2,18},{18,2},{3,19},{19,3},{4,20},{20... | collective-permute-start | bytes 270344 | tf_op jit(solution)/shard_map/ppermute | solution.py:29
  36.7 3.9 %collective-permute-start.6 = (f32[7,8,128]{2,1,0:T(8,128)S(1)}, f32[7,8,128]{2,1,0:T(8,128)S(1)}, u32[]{:S(2)}, u32[]{:S(2)}) collective-permute-start(f32[7,8,128]{2,1,0:T(8,128)S(1)} %get-tuple-element.20), channel_id=1, source_target_pairs={{0,3},{1,0},{2,1},{3,2},{4,7},{5,4},{6,5},{7,6},{8,11},{9,8},{10,9... | collective-permute-start | bytes 86024 | tf_op jit(solution)/shard_map/ppermute | solution.py:29
  38.7 5.4 %collective-permute-start.7 = (f32[7,8,128]{2,1,0:T(8,128)S(1)}, f32[7,8,128]{2,1,0:T(8,128)S(1)}, u32[]{:S(2)}, u32[]{:S(2)}) collective-permute-start(f32[7,8,128]{2,1,0:T(8,128)S(1)} %get-tuple-element.19), channel_id=1, source_target_pairs={{0,12},{4,0},{8,4},{12,8},{1,13},{5,1},{9,5},{13,9},{2,14},{6,2},{... | collective-permute-start | bytes 86024 | tf_op jit(solution)/shard_map/ppermute | solution.py:29
  39.7 3.4 %collective-permute-start.5 = (f32[72,128]{1,0:T(8,128)S(1)}, f32[72,128]{1,0:T(8,128)S(1)}, u32[]{:S(2)}, u32[]{:S(2)}) collective-permute-start(f32[72,128]{1,0:T(8,128)S(1)} %pad_maximum_fusion.2), channel_id=1, source_target_pairs={{0,4},{4,8},{8,12},{12,0},{1,5},{5,9},{9,13},{13,1},{2,6},{6,10},{... | collective-permute-start | bytes 110600 | tf_op jit(solution)/shard_map/ppermute | solution.py:29
  44.0 0.7 %copy-start.7 = (f32[6,7,8,128]{3,2,1,0:T(8,128)}, f32[6,7,8,128]{3,2,1,0:T(8,128)S(1)}, u32[]{:S(2)}) copy-start(f32[6,7,8,128]{3,2,1,0:T(8,128)S(1)} %bitcast_dynamic-update-slice_fusion) | copy-start | bytes 516100
where the time goes:
time: 44.9 us; the launch traced here: 44.7 us
  waiting for transfers between devices  15.7 us (35%)
  Pallas kernels  14.3 us (32%)
  starting transfers between devices  11.6 us (26%)
  local copies, waits for them, and re-layouts  2.35 us (5%)
  between operations  0.77 us (2%)
    ppermute x8, waiting for transfers between devices, moved_along(): lax.ppermute(block, axis, [(i, (i + distance) % count) for i in range(cou...  15.7 us
    pallas_call x6, Pallas kernels, call(): pl.pallas_call(body, out_shape=[jax.ShapeDtypeStruct(shape, jnp.float32)...  14.3 us
    ppermute x8, starting transfers between devices, moved_along(): lax.ppermute(block, axis, [(i, (i + distance) % count) for i in range(cou...  11.6 us
    unnamed x19, local copies, waits for them, and re-layouts  2.32 us
  transfers between devices with their start and end apart: 8, of which 7 were waited for; matrix products, arithmetic and copies ran while one was open for 0% of the time, Pallas kernels for 2%

commit v1 on v0

--- a/solution.py
+++ b/solution.py
@@ -18,7 +18,7 @@
 PACK = 32
 HEAD = 8
 ROWS_Y = 24
-UNROLL = 4
+UNROLL = 8
 
 VMEM = pl.BlockSpec(memory_space=pltpu.VMEM)
 SMEM = pl.BlockSpec(memory_space=pltpu.SMEM)
@@ -27,6 +27,12 @@
 def moved_along(block, axis, distance):
     count = lax.axis_size(axis)
     return lax.ppermute(block, axis, [(i, (i + distance) % count) for i in range(count)])
+
+
+def moved_inside(block, axis, distance):
+    count = lax.axis_size(axis)
+    route = [(i, i + distance) for i in range(count) if 0 <= i + distance < count]
+    return lax.ppermute(block, axis, route)
 
 
 def call(body, outs, *operands, smem=(), scratch=(), aliases=None, cost=None):
@@ -78,7 +84,7 @@
     loading, brick_ref, crossing_ref, gas_ref, face_ref, from_x_ref, from_y_ref,
     velocity_ref, fraction_ref, response_ref, cell_ref,
     moved_ref, base_ref, to_y_ref, to_x_ref, to_z_ref, out_ref,
-    grid_ref, deposit_ref, weight_ref, rows_ref,
+    grid_ref, deposit_ref, weight_ref, rows_ref, drag_ref,
 ):
     comps, size_x, size_y, size_z = gas_ref.shape
     nblocks = velocity_ref.shape[1]
@@ -131,30 +137,65 @@
     rows_ref[4] = high_main
     rows_ref[5] = high - high_main
     rows_ref[6] = 1.0 / response_ref[...]
+    rows_ref[7] = low
+    rows_ref[8] = high
 
     packed_z = lax.broadcasted_iota(jnp.int32, (16, LANES), 0).astype(jnp.float32).astype(jnp.bfloat16)
     sub_y = sub.astype(jnp.float32)
     last = count_z - 1
-
-    def one(k):
+    offsets = [(c * (size_x + 1) + a) * ROWS_Y for c in range(comps) for a in range(reach_x)]
+
+    def row(i, k):
+        return rows_ref[i, pl.ds(k, 1)]
+
+    def spot_of(k):
         brick = brick_ref[k]
         brick_x = brick // (count_y * count_z)
         brick_y = brick // count_z % count_y
         brick_z = brick % count_z
         sel = jnp.where(brick_z == last, 1, 0)
         start = HEAD + (sel * comps * (size_x + 1) + brick_x * BX) * ROWS_Y + brick_y * BY
-
-        def row(i):
-            return rows_ref[i, pl.ds(k, 1)]
+        return start, brick_z * BZ
+
+    def weight_y_of(k):
+        in_y, along_y = row(0, k), fraction_ref[1, pl.ds(k, 1)]
+        return jnp.where(sub_y == in_y, 1.0 - along_y, 0.0) + jnp.where(sub_y == in_y + 1.0, along_y, 0.0)
+
+    def drag_of(k):
+        start, first_z = spot_of(k)
+        place = cell_ref[pl.ds(k, 1)] % BZ + first_z
+        place = jnp.broadcast_to(place, (reach_y, LANES))
+        after = (place + 1) % size_z
+        low, high = row(7, k), row(8, k)
+        weight_x = [weight_ref[a, pl.ds(k, 1)] for a in range(reach_x)]
+        weight_low = [w * low for w in weight_x]
+        weight_high = [w * high for w in weight_x]
+        weight_y = weight_y_of(k)
+        rate = row(6, k)
+        for c in range(comps):
+            total = None
+            for a in range(reach_x):
+                window = grid_ref[pl.ds(start + offsets[c * reach_x + a], reach_y)]
+                one = jnp.take_along_axis(window, place, axis=1, mode="promise_in_bounds") * weight_low[a]
+                two = jnp.take_along_axis(window, after, axis=1, mode="promise_in_bounds") * weight_high[a]
+                total = one + two if total is None else total + (one + two)
+            gas_sample = jnp.sum(total * weight_y, axis=0, keepdims=True)
+            moving = velocity_ref[c, pl.ds(k, 1)]
+            drag = (gas_sample - moving) * rate
+            moved_ref[c, pl.ds(k, 1)] = moving + TIME_STEP * drag
+            drag_ref[c, pl.ds(k, 1)] = drag
+
+    def shares_of(k):
+        start, first_z = spot_of(k)
 
         def tall(value):
             return jnp.broadcast_to(value, (16, LANES)).astype(jnp.bfloat16)
 
-        place = row(1) + (brick_z * BZ).astype(jnp.float32)
+        place = row(1, k) + first_z.astype(jnp.float32)
         after = place + 1.0
         after = jnp.where(after == float(size_z), 0.0, after)
         place, after = tall(place), tall(after)
-        low_main, low_rest, high_main, high_rest = [tall(row(i)) for i in (2, 3, 4, 5)]
+        low_main, low_rest, high_main, high_rest = [tall(row(i, k)) for i in (2, 3, 4, 5)]
         nothing = jnp.zeros((16, LANES), jnp.bfloat16)
         main, rest = [], []
         for j in range(size_z // 16):
@@ -162,45 +203,29 @@
             at_low, at_high = here == place, here == after
             main.append(jnp.where(at_low, low_main, jnp.where(at_high, high_main, nothing)))
             rest.append(jnp.where(at_low, low_rest, jnp.where(at_high, high_rest, nothing)))
-        main, rest = jnp.concatenate(main, axis=0), jnp.concatenate(rest, axis=0)
-        both = jnp.concatenate([main, rest], axis=1)
-        table = jnp.concatenate([both, both], axis=0)
-        both_t = jnp.concatenate([main, rest], axis=0)
-        table_t = jnp.concatenate([both_t, both_t], axis=1)
-
-        def cut(value):
-            top = value.astype(jnp.bfloat16)
-            return jnp.concatenate([top, (value - top.astype(jnp.float32)).astype(jnp.bfloat16)], axis=1)
-
-        offsets = [(c * (size_x + 1) + a) * ROWS_Y for c in range(comps) for a in range(reach_x)]
-        window = jnp.concatenate([grid_ref[pl.ds(start + o, reach_y)] for o in offsets], axis=0)
-        lines = lax.dot_general(cut(window), table, (((1,), (0,)), ((), ())), preferred_element_type=jnp.float32)
-        lines = lines[:, :LANES] + lines[:, LANES:]
-        lines = lines.reshape(comps, reach_x, reach_y, LANES)
+        both = jnp.concatenate(main + rest, axis=0)
+        table = jnp.concatenate([both, both], axis=1)
         weight_x = [weight_ref[a, pl.ds(k, 1)] for a in range(reach_x)]
-        in_y, along_y = row(0), fraction_ref[1, pl.ds(k, 1)]
-        weight_y = jnp.where(sub_y == in_y, 1.0 - along_y, 0.0) + jnp.where(sub_y == in_y + 1.0, along_y, 0.0)
-        rate = row(6)
+        weight_y = weight_y_of(k)
         pushed = []
         for c in range(comps):
-            total = lines[c, 0] * weight_x[0]
-            for a in range(1, reach_x):
-                total = total + lines[c, a] * weight_x[a]
-            gas_sample = jnp.sum(total * weight_y, axis=0, keepdims=True)
-            moving = velocity_ref[c, pl.ds(k, 1)]
-            drag = (gas_sample - moving) * rate
-            moved_ref[c, pl.ds(k, 1)] = moving + TIME_STEP * drag
-            spread = drag * weight_y
+            spread = drag_ref[c, pl.ds(k, 1)] * weight_y
             pushed.extend(spread * weight_x[a] for a in range(reach_x))
         pushed = jnp.concatenate(pushed, axis=0)
-        shares = lax.dot_general(cut(pushed), table_t, (((1,), (1,)), ((), ())), preferred_element_type=jnp.float32)
-        shares = shares[:, :LANES] + shares[:, LANES:]
-        return start, offsets, shares
+        top = pushed.astype(jnp.bfloat16)
+        pushed = jnp.concatenate([top, (pushed - top.astype(jnp.float32)).astype(jnp.bfloat16)], axis=1)
+        shares = lax.dot_general(pushed, table, (((1,), (1,)), ((), ())), preferred_element_type=jnp.float32)
+        return start, shares[:, :LANES] + shares[:, LANES:]
 
     @pl.loop(0, nblocks // UNROLL)
     def _(group):
-        results = [one(group * UNROLL + u) for u in range(UNROLL)]
-        for start, offsets, shares in results:
+        for u in range(UNROLL):
+            drag_of(group * UNROLL + u)
+
+    @pl.loop(0, nblocks // UNROLL)
+    def _(group):
+        results = [shares_of(group * UNROLL + u) for u in range(UNROLL)]
+        for start, shares in results:
             for i, o in enumerate(offsets):
                 spot = pl.ds(start + o, reach_y)
                 deposit_ref[spot] = deposit_ref[spot] + shares[i * reach_y : (i + 1) * reach_y]
@@ -303,7 +328,7 @@
     from_x = moved_along(plane, "gx", -1)
     rows = -(-(comps * size_x + comps + 1) // 8) * 8
     (lines,) = call(halo_y_kernel, [(rows, LANES)], gas_field, face, from_x)
-    from_y = moved_along(lines, "gy", -1)
+    from_y = moved_inside(lines, "gy", -1)
 
     grid_rows = HEAD + 2 * comps * (size_x + 1) * ROWS_Y
     moved, base, to_y, to_x, to_z, leaving = call(
@@ -322,7 +347,8 @@
             pltpu.VMEM((grid_rows, LANES), jnp.float32),
             pltpu.VMEM((grid_rows, LANES), jnp.float32),
             pltpu.VMEM((BX + 1, nblocks, LANES), jnp.float32),
-            pltpu.VMEM((7, nblocks, LANES), jnp.float32),
+            pltpu.VMEM((9, nblocks, LANES), jnp.float32),
+            pltpu.VMEM((comps, nblocks, LANES), jnp.float32),
         ),
     )
 
@@ -333,8 +359,8 @@
         return jnp.concatenate([flat(array) for array in arrays], axis=0)
 
     count = flat(leaving[0]).shape[0]
-    got_y = moved_along(joined(to_y, leaving[2]), "gy", 1)
-    got_my = moved_along(leaving[3], "gy", -1)
+    got_y = moved_inside(joined(to_y, leaving[2]), "gy", 1)
+    got_my = moved_inside(leaving[3], "gy", -1)
     got_mz = moved_along(leaving[5], "gz", -1)
     edge = comps * size_y
     x_part, z_part = call(

time: 44.9 us -> 44 us (0.980)
  Pallas kernels: 14.3 us -> 13.7 us
  waiting for transfers between devices: 15.7 us -> 15.1 us
    ppermute x8 -> x5, waiting for transfers between devices: 15.7 us -> 5.81 us  [moved_along(): lax.ppermute(block, axis, [(i, (i + distance) % count) for i in range(cou...]
    ppermute x0 -> x3, waiting for transfers between devices: none -> 9.29 us  [moved_inside(): return lax.ppermute(block, axis, route)]
    ppermute x0 -> x3, starting transfers between devices: none -> 6.06 us  [moved_inside(): return lax.ppermute(block, axis, route)]
    ppermute x8 -> x5, starting transfers between devices: 11.6 us -> 5.65 us  [moved_along(): lax.ppermute(block, axis, [(i, (i + distance) % count) for i in range(cou...]
    pallas_call x6, Pallas kernels: 14.3 us -> 13.7 us  [call(): pl.pallas_call(body, out_shape=[jax.ShapeDtypeStruct(shape, jnp.float32)...]
where the time goes in v1:
time: 44 us; the launch traced here: 43.8 us
  waiting for transfers between devices  15.1 us (34%)
  Pallas kernels  13.7 us (31%)
  starting transfers between devices  11.7 us (27%)
  local copies, waits for them, and re-layouts  2.35 us (5%)
  between operations  0.81 us (2%)
    pallas_call x6, Pallas kernels, call(): pl.pallas_call(body, out_shape=[jax.ShapeDtypeStruct(shape, jnp.float32)...  13.7 us
    ppermute x3, waiting for transfers between devices, moved_inside(): return lax.ppermute(block, axis, route)  9.29 us
    ppermute x3, starting transfers between devices, moved_inside(): return lax.ppermute(block, axis, route)  6.06 us
    ppermute x5, waiting for transfers between devices, moved_along(): lax.ppermute(block, axis, [(i, (i + distance) % count) for i in range(cou...  5.81 us
    ppermute x5, starting transfers between devices, moved_along(): lax.ppermute(block, axis, [(i, (i + distance) % count) for i in range(cou...  5.65 us
    unnamed x19, local copies, waits for them, and re-layouts  2.32 us
  transfers between devices with their start and end apart: 8, of which 7 were waited for; matrix products, arithmetic and copies ran while one was open for 0% of the time, Pallas kernels for 2%

profile of v1, /device:TPU:0, one launch (start us, length us, event | category | flops | bytes accessed | tf_op | source)
XLA Modules:
  0.0 43.8 jit_solution(1078948115446065448)
XLA Ops:
  0.6 0.0 copy-start
  0.6 1.0 %copy-done = f32[3,16,16,128]{3,2,1,0:T(8,128)S(1)} copy-done((f32[3,16,16,128]{3,2,1,0:T(8,128)S(1)}, f32[3,16,16,128]{3,2,1,0:T(8,128)}, u32[]{:S(2)}) %copy-start) | copy-done | bytes 393240
  1.6 0.2 shard_map.94
  1.8 0.0 slice-start
  1.8 2.4 %collective-permute-start = (f32[16,128]{1,0:T(8,128)S(1)}, f32[16,128]{1,0:T(8,128)S(1)}, u32[]{:S(2)}, u32[]{:S(2)}) collective-permute-start(f32[16,128]{1,0:T(8,128)S(1)} %shard_map.94), channel_id=1, source_target_pairs={{0,12},{4,0},{8,4},{12,8},{1,13},{5,1},{9,5},{13,9},{2,14},{6,2},{... | collective-permute-start | bytes 24584 | tf_op jit(solution)/shard_map/ppermute | solution.py:29
  4.2 1.4 %collective-permute-done.face_ref = f32[16,128]{1,0:T(8,128)S(1)} collective-permute-done((f32[16,128]{1,0:T(8,128)S(1)}, f32[16,128]{1,0:T(8,128)S(1)}, u32[]{:S(2)}, u32[]{:S(2)}) %collective-permute-start) | collective-permute-done | bytes 8224 | tf_op jit(solution)/shard_map/ppermute | solution.py:29
  5.6 0.0 slice-done
  5.6 0.0 copy-start.1
  5.6 0.0 copy-start.2
  5.6 0.0 copy-start.3
  5.6 0.0 copy-start.4
  5.6 1.6 %collective-permute-start.1 = (f32[64,128]{1,0:T(8,128)S(1)}, f32[64,128]{1,0:T(8,128)S(1)}, u32[]{:S(2)}, u32[]{:S(2)}) collective-permute-start(f32[64,128]{1,0:T(8,128)S(1)} %pad_maximum_fusion.3), channel_id=1, source_target_pairs={{0,16},{16,0},{1,17},{17,1},{2,18},{18,2},{3,19},{19,3},{4,20},{20... | collective-permute-start | bytes 98312 | tf_op jit(solution)/shard_map/ppermute | solution.py:29
  7.2 2.4 %collective-permute-done.1.from_x_ref = f32[64,128]{1,0:T(8,128)S(1)} collective-permute-done((f32[64,128]{1,0:T(8,128)S(1)}, f32[64,128]{1,0:T(8,128)S(1)}, u32[]{:S(2)}, u32[]{:S(2)}) %collective-permute-start.1) | collective-permute-done | bytes 32800 | tf_op jit(solution)/shard_map/ppermute | solution.py:29
  9.7 0.0 copy-start.5
  9.7 0.1 shard_map.95
  9.7 1.3 %collective-permute-start.2 = (f32[56,128]{1,0:T(8,128)S(1)}, f32[56,128]{1,0:T(8,128)S(1)}, u32[]{:S(2)}, u32[]{:S(2)}) collective-permute-start(f32[56,128]{1,0:T(8,128)S(1)} %shard_map.95), channel_id=1, source_target_pairs={{1,0},{2,1},{3,2},{5,4},{6,5},{7,6},{9,8},{10,9},{11,10},{13,12},{... | collective-permute-start | bytes 86024 | tf_op jit(solution)/shard_map/ppermute | solution.py:35
  11.0 4.5 %collective-permute-done.2.from_y_ref = f32[56,128]{1,0:T(8,128)S(1)} collective-permute-done((f32[56,128]{1,0:T(8,128)S(1)}, f32[56,128]{1,0:T(8,128)S(1)}, u32[]{:S(2)}, u32[]{:S(2)}) %collective-permute-start.2) | collective-permute-done | bytes 28704 | tf_op jit(solution)/shard_map/ppermute | solution.py:35
  15.5 0.0 copy-start.6
  15.5 0.0 copy-done.1
  15.5 0.0 copy-done.2
  15.5 0.0 copy-done.3
  15.5 0.0 copy-done.4
  15.5 0.0 copy-done.5
  15.5 0.6 %copy-done.6 = s32[64]{0:T(128)S(1)} copy-done((s32[64]{0:T(128)S(1)}, s32[64]{0:T(128)}, u32[]{:S(2)}) %copy-start.6) | copy-done | bytes 280
  16.1 12.5 %shard_map.96 = (f32[3,64,128]{2,1,0:T(8,128)}, f32[3,16,16,128]{3,2,1,0:T(8,128)S(1)}, f32[72,128]{1,0:T(8,128)S(1)}, f32[48,128]{1,0:T(8,128)S(1)}, f32[16,128...) custom-call(s32[64]{0:T(128)S(1)} %copy-done.6, s32[6,8]{1,0:T(8,128)S(1)} %copy-done.5, f32[3,16,16,128]{3,2,1,0:T(8,128)S(1)} %copy-done, ...), custom_call_target="tpu_custom_call" | custom-call | tf_op jit(solution)/shard_map/pallas_call | solution.py:39
  28.7 3.5 %collective-permute-start.3 = (f32[128,128]{1,0:T(8,128)S(1)}, f32[128,128]{1,0:T(8,128)S(1)}, u32[]{:S(2)}, u32[]{:S(2)}) collective-permute-start(f32[128,128]{1,0:T(8,128)S(1)} %pad_maximum_fusion.1), channel_id=1, source_target_pairs={{0,1},{1,2},{2,3},{4,5},{5,6},{6,7},{8,9},{9,10},{10,11},{12,13},{... | collective-permute-start | bytes 196616 | tf_op jit(solution)/shard_map/ppermute | solution.py:35
  32.2 1.9 %collective-permute-done.3.from_y_ref = f32[128,128]{1,0:T(8,128)S(1)} collective-permute-done((f32[128,128]{1,0:T(8,128)S(1)}, f32[128,128]{1,0:T(8,128)S(1)}, u32[]{:S(2)}, u32[]{:S(2)}) %collective-permute-start.3) | collective-permute-done | bytes 65568 | tf_op jit(solution)/shard_map/ppermute | solution.py:35
  34.1 1.6 %collective-permute-start.4 = (f32[176,128]{1,0:T(8,128)S(1)}, f32[176,128]{1,0:T(8,128)S(1)}, u32[]{:S(2)}, u32[]{:S(2)}) collective-permute-start(f32[176,128]{1,0:T(8,128)S(1)} %pad_maximum_fusion), channel_id=1, source_target_pairs={{0,16},{16,0},{1,17},{17,1},{2,18},{18,2},{3,19},{19,3},{4,20},{20... | collective-permute-start | bytes 270344 | tf_op jit(solution)/shard_map/ppermute | solution.py:29
  35.7 1.3 %collective-permute-start.6 = (f32[7,8,128]{2,1,0:T(8,128)S(1)}, f32[7,8,128]{2,1,0:T(8,128)S(1)}, u32[]{:S(2)}, u32[]{:S(2)}) collective-permute-start(f32[7,8,128]{2,1,0:T(8,128)S(1)} %get-tuple-element.20), channel_id=1, source_target_pairs={{1,0},{2,1},{3,2},{5,4},{6,5},{7,6},{9,8},{10,9},{11,10},{13,12},{... | collective-permute-start | bytes 86024 | tf_op jit(solution)/shard_map/ppermute | solution.py:35
  37.0 0.1 collective-permute-start.7
  37.1 1.6 %collective-permute-done.4.from_x_ref = f32[176,128]{1,0:T(8,128)S(1)} collective-permute-done((f32[176,128]{1,0:T(8,128)S(1)}, f32[176,128]{1,0:T(8,128)S(1)}, u32[]{:S(2)}, u32[]{:S(2)}) %collective-permute-start.4) | collective-permute-done | bytes 90144 | tf_op jit(solution)/shard_map/ppermute | solution.py:29
  38.7 0.1 shard_map.98
  38.8 0.0 collective-permute-start.5
  38.8 3.0 %collective-permute-done.6 = f32[7,8,128]{2,1,0:T(8,128)S(1)} collective-permute-done((f32[7,8,128]{2,1,0:T(8,128)S(1)}, f32[7,8,128]{2,1,0:T(8,128)S(1)}, u32[]{:S(2)}, u32[]{:S(2)}) %collective-permute-start.6) | collective-permute-done | bytes 28704 | tf_op jit(solution)/shard_map/ppermute | solution.py:35
  41.8 0.4 collective-permute-done.5
  42.2 0.9 %shard_map.99 = f32[3,16,16,128]{3,2,1,0:T(8,128)} custom-call(f32[3,16,16,128]{3,2,1,0:T(8,128)S(1)} %get-tuple-element.11.base_ref, f32[72,128]{1,0:T(8,128)S(1)} %slice.56.from_y_ref, f32[48,128]{1,0:T(8,128)S(1)} %slice.57.from_x_ref, f32[16,128]{1,0:T(8,128)S(1)} %slice.58.from_z_ref), custom_call_target="tpu_custom_call" | custom-call | tf_op jit(solution)/shard_map/pallas_call | solution.py:39
  43.1 0.0 collective-permute-done.7
  43.1 0.0 copy-start.7
  43.1 0.7 %copy-done.7 = f32[6,7,8,128]{3,2,1,0:T(8,128)} copy-done((f32[6,7,8,128]{3,2,1,0:T(8,128)}, f32[6,7,8,128]{3,2,1,0:T(8,128)S(1)}, u32[]{:S(2)}) %copy-start.7) | copy-done | bytes 172056
  (16 shorter events, 0.1 us)
Async XLA Ops:
  0.6 1.0 %copy-start = (f32[3,16,16,128]{3,2,1,0:T(8,128)S(1)}, f32[3,16,16,128]{3,2,1,0:T(8,128)}, u32[]{:S(2)}) copy-start(f32[3,16,16,128]{3,2,1,0:T(8,128)} %gas_ref.5) | copy-start | bytes 1179652
  1.8 3.8 %slice-start = ((f32[3,16,16,128]{3,2,1,0:T(8,128)}), f32[3,1,16,128]{3,2,1,0:T(8,128)S(1)}, s32[]{:S(2)}) async-start(f32[3,16,16,128]{3,2,1,0:T(8,128)} %gas_ref.5), calls=%async_computation | async-start | bytes 49152 | tf_op jit(solution)/shard_map/slice | solution.py:327
  1.8 3.8 %collective-permute-start = (f32[16,128]{1,0:T(8,128)S(1)}, f32[16,128]{1,0:T(8,128)S(1)}, u32[]{:S(2)}, u32[]{:S(2)}) collective-permute-start(f32[16,128]{1,0:T(8,128)S(1)} %shard_map.94), channel_id=1, source_target_pairs={{0,12},{4,0},{8,4},{12,8},{1,13},{5,1},{9,5},{13,9},{2,14},{6,2},{... | collective-permute-start | bytes 24584 | tf_op jit(solution)/shard_map/ppermute | solution.py:29
  5.6 9.9 %copy-start.1 = (f32[64,3,128]{2,0,1:T(8,128)S(1)}, f32[64,3,128]{2,0,1:T(8,128)}, u32[]{:S(2)}) copy-start(f32[64,3,128]{2,0,1:T(8,128)} %param.8) | copy-start | bytes 294916
  5.6 9.9 %copy-start.2 = (f32[64,3,128]{2,0,1:T(8,128)S(1)}, f32[64,3,128]{2,0,1:T(8,128)}, u32[]{:S(2)}) copy-start(f32[64,3,128]{2,0,1:T(8,128)} %param.9) | copy-start | bytes 294916
  5.6 9.9 %copy-start.3 = (f32[64,128]{1,0:T(8,128)S(1)}, f32[64,128]{1,0:T(8,128)}, u32[]{:S(2)}) copy-start(f32[64,128]{1,0:T(8,128)} %response_ref.1) | copy-start | bytes 98308
  5.6 9.9 %copy-start.4 = (s32[64,128]{1,0:T(8,128)S(1)}, s32[64,128]{1,0:T(8,128)}, u32[]{:S(2)}) copy-start(s32[64,128]{1,0:T(8,128)} %cell_ref.1) | copy-start | bytes 98308
  5.6 4.0 %collective-permute-start.1 = (f32[64,128]{1,0:T(8,128)S(1)}, f32[64,128]{1,0:T(8,128)S(1)}, u32[]{:S(2)}, u32[]{:S(2)}) collective-permute-start(f32[64,128]{1,0:T(8,128)S(1)} %pad_maximum_fusion.3), channel_id=1, source_target_pairs={{0,16},{16,0},{1,17},{17,1},{2,18},{18,2},{3,19},{19,3},{4,20},{20... | collective-permute-start | bytes 98312 | tf_op jit(solution)/shard_map/ppermute | solution.py:29
  9.7 5.9 %copy-start.5 = (s32[6,8]{1,0:T(8,128)S(1)}, s32[6,8]{1,0:T(8,128)}, u32[]{:S(2)}) copy-start(s32[6,8]{1,0:T(8,128)} %crossing_ref.1) | copy-start | bytes 580
  9.7 5.8 %collective-permute-start.2 = (f32[56,128]{1,0:T(8,128)S(1)}, f32[56,128]{1,0:T(8,128)S(1)}, u32[]{:S(2)}, u32[]{:S(2)}) collective-permute-start(f32[56,128]{1,0:T(8,128)S(1)} %shard_map.95), channel_id=1, source_target_pairs={{1,0},{2,1},{3,2},{5,4},{6,5},{7,6},{9,8},{10,9},{11,10},{13,12},{... | collective-permute-start | bytes 86024 | tf_op jit(solution)/shard_map/ppermute | solution.py:35
  15.5 0.7 %copy-start.6 = (s32[64]{0:T(128)S(1)}, s32[64]{0:T(128)}, u32[]{:S(2)}) copy-start(s32[64]{0:T(128)} %brick_ref.1) | copy-start | bytes 772
  28.7 5.4 %collective-permute-start.3 = (f32[128,128]{1,0:T(8,128)S(1)}, f32[128,128]{1,0:T(8,128)S(1)}, u32[]{:S(2)}, u32[]{:S(2)}) collective-permute-start(f32[128,128]{1,0:T(8,128)S(1)} %pad_maximum_fusion.1), channel_id=1, source_target_pairs={{0,1},{1,2},{2,3},{4,5},{5,6},{6,7},{8,9},{9,10},{10,11},{12,13},{... | collective-permute-start | bytes 196616 | tf_op jit(solution)/shard_map/ppermute | solution.py:35
  34.1 4.6 %collective-permute-start.4 = (f32[176,128]{1,0:T(8,128)S(1)}, f32[176,128]{1,0:T(8,128)S(1)}, u32[]{:S(2)}, u32[]{:S(2)}) collective-permute-start(f32[176,128]{1,0:T(8,128)S(1)} %pad_maximum_fusion), channel_id=1, source_target_pairs={{0,16},{16,0},{1,17},{17,1},{2,18},{18,2},{3,19},{19,3},{4,20},{20... | collective-permute-start | bytes 270344 | tf_op jit(solution)/shard_map/ppermute | solution.py:29
  35.7 6.1 %collective-permute-start.6 = (f32[7,8,128]{2,1,0:T(8,128)S(1)}, f32[7,8,128]{2,1,0:T(8,128)S(1)}, u32[]{:S(2)}, u32[]{:S(2)}) collective-permute-start(f32[7,8,128]{2,1,0:T(8,128)S(1)} %get-tuple-element.20), channel_id=1, source_target_pairs={{1,0},{2,1},{3,2},{5,4},{6,5},{7,6},{9,8},{10,9},{11,10},{13,12},{... | collective-permute-start | bytes 86024 | tf_op jit(solution)/shard_map/ppermute | solution.py:35
  37.0 6.1 %collective-permute-start.7 = (f32[7,8,128]{2,1,0:T(8,128)S(1)}, f32[7,8,128]{2,1,0:T(8,128)S(1)}, u32[]{:S(2)}, u32[]{:S(2)}) collective-permute-start(f32[7,8,128]{2,1,0:T(8,128)S(1)} %get-tuple-element.19), channel_id=1, source_target_pairs={{0,12},{4,0},{8,4},{12,8},{1,13},{5,1},{9,5},{13,9},{2,14},{6,2},{... | collective-permute-start | bytes 86024 | tf_op jit(solution)/shard_map/ppermute | solution.py:29
  38.8 3.4 %collective-permute-start.5 = (f32[72,128]{1,0:T(8,128)S(1)}, f32[72,128]{1,0:T(8,128)S(1)}, u32[]{:S(2)}, u32[]{:S(2)}) collective-permute-start(f32[72,128]{1,0:T(8,128)S(1)} %pad_maximum_fusion.2), channel_id=1, source_target_pairs={{0,4},{4,8},{8,12},{12,0},{1,5},{5,9},{9,13},{13,1},{2,6},{6,10},{... | collective-permute-start | bytes 110600 | tf_op jit(solution)/shard_map/ppermute | solution.py:29
  43.1 0.7 %copy-start.7 = (f32[6,7,8,128]{3,2,1,0:T(8,128)}, f32[6,7,8,128]{3,2,1,0:T(8,128)S(1)}, u32[]{:S(2)}) copy-start(f32[6,7,8,128]{3,2,1,0:T(8,128)S(1)} %bitcast_dynamic-update-slice_fusion) | copy-start | bytes 516100

commit v2 on v1

v2 whole, which is shorter than its diff:
```python
import functools

import jax
import jax.numpy as jnp
from jax import lax
from jax.experimental import pallas as pl
from jax.experimental.pallas import tpu as pltpu
from jax.sharding import PartitionSpec as P

BX = 4
BY = 4
BZ = 8

TIME_STEP = 0.25
VISCOSITY = 0.4

LANES = 128
PACK = 32
HEAD = 8
ROWS_Y = 24
REACH_X = BX + 1
REACH_Y = 8
UNROLL = 8

LOW, HIGH, WEIGHT, ALONG_Y, IN_Y, IN_Z = 0, 5, 10, 15, 16, 17
LOW_MAIN, LOW_REST, HIGH_MAIN, HIGH_REST, RATE, MOVING = 18, 19, 20, 21, 22, 23
TABLE_ROWS = 26

VMEM = pl.BlockSpec(memory_space=pltpu.VMEM)
SMEM = pl.BlockSpec(memory_space=pltpu.SMEM)


def moved_along(block, axis, distance):
    count = lax.axis_size(axis)
    return lax.ppermute(block, axis, [(i, (i + distance) % count) for i in range(count)])


def swapped(blocks, axis, periodic):
    count = lax.axis_size(axis)
    first = [(i, i ^ 1) for i in range(count)]
    second = [(i, (((i + 1) ^ 1) - 1) % count) for i in range(count)]
    if not periodic:
        second[0], second[-1] = (0, 0), (count - 1, count - 1)
    return lax.ppermute(blocks[0], axis, first), lax.ppermute(blocks[1], axis, second)


def moved_diagonally(block, distance):
    nx, nz = lax.axis_size("gx"), lax.axis_size("gz")
    route = [(i * nz + k, (i + distance) % nx * nz + (k + distance) % nz) for i in range(nx) for k in range(nz)]
    return lax.ppermute(block, ("gx", "gz"), route)


def call(body, outs, *operands, smem=(), smem_outs=(), scratch=(), aliases=None, cycles=0):
    return pl.pallas_call(
        body,
        out_shape=[o if isinstance(o, jax.ShapeDtypeStruct) else jax.ShapeDtypeStruct(o, jnp.float32) for o in outs],
        in_specs=[SMEM if i in smem else VMEM for i in range(len(operands))],
        out_specs=[SMEM if i in smem_outs else VMEM for i in range(len(outs))],
        scratch_shapes=list(scratch),
        input_output_aliases=aliases or {},
        compiler_params=pltpu.CompilerParams(vmem_limit_bytes=40 * 1024 * 1024),
        cost_estimate=pl.CostEstimate(flops=cycles * 4096, bytes_accessed=cycles * 1024, transcendentals=0),
    )(*operands)


def lane_ids(rows):
    return lax.broadcasted_iota(jnp.int32, (rows, LANES), 1)


def row_ids(rows):
    return lax.broadcasted_iota(jnp.int32, (rows, LANES), 0)


def turned(value, shift):
    shift = shift % LANES
    return pltpu.roll(value, shift, 1) if shift else value


def row_of(sel, c, x, comps, size_x):
    return HEAD + ((sel * comps + c) * (size_x + 1) + x) * ROWS_Y


def odd(axis):
    return lax.axis_index(axis) % 2


def pack_face_kernel(gas_ref, face_ref):
    comps, size_x, size_y, _ = gas_ref.shape
    lane = lane_ids(size_y)
    face = jnp.zeros((size_y, LANES), jnp.float32)
    for c in range(comps):
        for x in range(size_x):
            place = PACK * c + x
            face = jnp.where(lane == place, turned(gas_ref[c, x], place), face)
    face_ref[...] = face


def prepare_kernel(
    gas_ref, velocity_ref, fraction_ref, response_ref, cell_ref, brick_ref,
    grid_ref, deposit_ref, table_ref, list_ref,
):
    comps, size_x, size_y, size_z = gas_ref.shape
    nblocks = velocity_ref.shape[1]
    count_y, count_z = size_y // BY, size_z // BZ
    spare = table_ref.shape[1] - nblocks

    cells = cell_ref[...]
    cell_x, cell_y, cell_z = cells // (BY * BZ), cells // BZ % BY, cells % BZ
    along_x, along_z = fraction_ref[0], fraction_ref[2]
    low, high = 1.0 - along_z, along_z

    def put(row, value):
        table_ref[row, 0:nblocks] = value
        table_ref[row, nblocks : nblocks + spare] = jnp.zeros((spare, LANES), jnp.float32)

    for a in range(REACH_X):
        weight = jnp.where(cell_x == a, 1.0 - along_x, 0.0) + jnp.where(cell_x == a - 1, along_x, 0.0)
        put(LOW + a, weight * low)
        put(HIGH + a, weight * high)
        put(WEIGHT + a, weight)
    put(ALONG_Y, fraction_ref[1])
    put(IN_Y, cell_y.astype(jnp.float32))
    put(IN_Z, cell_z.astype(jnp.float32))
    low_main = low.astype(jnp.bfloat16).astype(jnp.float32)
    high_main = high.astype(jnp.bfloat16).astype(jnp.float32)
    put(LOW_MAIN, low_main)
    put(LOW_REST, low - low_main)
    put(HIGH_MAIN, high_main)
    put(HIGH_REST, high - high_main)
    put(RATE, 1.0 / response_ref[...])
    for c in range(comps):
        put(MOVING + c, velocity_ref[c])

    room = nblocks + UNROLL

    def visit(k, counts):
        brick = brick_ref[k]
        brick_x = brick // (count_y * count_z)
        brick_y = brick // count_z % count_y
        brick_z = brick % count_z
        sel = jnp.where(brick_z == count_z - 1, 1, 0)
        late = jnp.where(brick_y == count_y - 1, 1, 0)
        at = jnp.where(late == 1, room + counts[1], counts[0])
        list_ref[0, at] = k
        list_ref[1, at] = HEAD + (sel * comps * (size_x + 1) + brick_x * BX) * ROWS_Y + brick_y * BY
        list_ref[2, at] = brick_z * BZ
        return counts[0] + 1 - late, counts[1] + late

    early, late = lax.fori_loop(0, nblocks, visit, (jnp.int32(0), jnp.int32(0)))
    for base, count in ((0, early), (room, late)):
        for u in range(UNROLL):
            list_ref[0, base + count + u] = nblocks
            list_ref[1, base + count + u] = HEAD
            list_ref[2, base + count + u] = 0
    list_ref[0, 2 * room] = early
    list_ref[0, 2 * room + 1] = late

    zeros = jnp.zeros((8, LANES), jnp.float32)
    grid_ref[0:HEAD] = zeros
    for c in range(comps):
        for x in range(size_x + 1):
            for sel in (0, 1):
                at = row_of(sel, c, x, comps, size_x)
                if x < size_x and sel == 0:
                    grid_ref[at : at + size_y] = gas_ref[c, x]
                grid_ref[at + size_y : at + ROWS_Y] = zeros
    deposit_ref[...] = jnp.zeros_like(deposit_ref)


def halo_xz_kernel(gas_ref, grid_in_ref, face_ref, from_x_ref, edge_ref, grid_ref, lines_ref):
    comps, size_x, size_y, _ = gas_ref.shape
    first_lane = lane_ids(size_y) == 0
    for c in range(comps):
        for x in range(size_x + 1):
            if x < size_x:
                plane, far = gas_ref[c, x], turned(face_ref[...], -(PACK * c + x))
                lines_ref[c * size_x + x : c * size_x + x + 1] = gas_ref[c, x, 0:1]
            else:
                plane = from_x_ref[c * size_y : (c + 1) * size_y]
                far = turned(edge_ref[...], -PACK * c)
                at = row_of(0, c, x, comps, size_x)
                grid_ref[at : at + size_y] = plane
                lines_ref[comps * size_x + c : comps * size_x + c + 1] = plane[0:1]
            at = row_of(1, c, x, comps, size_x)
            grid_ref[at : at + size_y] = jnp.where(first_lane, far, plane)
    line = jnp.where(lane_ids(8) % PACK == size_x, turned(edge_ref[0:8], size_x), face_ref[0:8])
    lines_ref[comps * size_x + comps : comps * size_x + comps + 1] = line[0:1]


def halo_y_kernel(comps, size_x, size_y, grid_in_ref, first_ref, second_ref, grid_ref):
    inside = lax.axis_index("gy") != lax.axis_size("gy") - 1
    even = odd("gy") == 0
    kept = (row_ids(8) == 0) & inside
    first_lane = lane_ids(8) == 0
    zeros = jnp.zeros((8, LANES), jnp.float32)

    def line_at(row):
        line = jnp.where(even, first_ref[row : row + 1], second_ref[row : row + 1])
        return jnp.broadcast_to(line, (8, LANES))

    corner = line_at(comps * size_x + comps)
    for c in range(comps):
        for x in range(size_x + 1):
            line = line_at(c * size_x + x if x < size_x else comps * size_x + c)
            at = row_of(0, c, x, comps, size_x) + size_y
            grid_ref[at : at + 8] = jnp.where(kept, line, zeros)
            at = row_of(1, c, x, comps, size_x) + size_y
            far = turned(corner, -(PACK * c + x))
            grid_ref[at : at + 8] = jnp.where(kept, jnp.where(first_lane, far, line), zeros)


def offsets_of(comps, size_x):
    return [(c * (size_x + 1) + a) * ROWS_Y for c in range(comps) for a in range(REACH_X)]


def weight_y_of(table_ref, k):
    along, inside = table_ref[ALONG_Y, pl.ds(k, 1)], table_ref[IN_Y, pl.ds(k, 1)]
    row = row_ids(REACH_Y).astype(jnp.float32)
    return jnp.where(row == inside, 1.0 - along, 0.0) + jnp.where(row == inside + 1.0, along, 0.0)


def drag_kernel(late, size_x, list_ref, grid_ref, table_ref, *refs):
    moved_ref, drag_ref = refs[-2:]
    comps, room = moved_ref.shape[0], (list_ref.shape[1] - 2) // 2
    offsets = offsets_of(comps, size_x)

    def one(k, start, first_z):
        def row(i):
            return table_ref[i, pl.ds(k, 1)]

        place = row(IN_Z).astype(jnp.int32) + first_z
        place = jnp.broadcast_to(place, (REACH_Y, LANES))
        after = (place + 1) % LANES
        low = [row(LOW + a) for a in range(REACH_X)]
        high = [row(HIGH + a) for a in range(REACH_X)]
        weight_y = weight_y_of(table_ref, k)
        rate = row(RATE)
        for c in range(comps):
            total = None
            for a in range(REACH_X):
                window = grid_ref[pl.ds(start + offsets[c * REACH_X + a], REACH_Y)]
                near = jnp.take_along_axis(window, place, axis=1, mode="promise_in_bounds") * low[a]
                far = jnp.take_along_axis(window, after, axis=1, mode="promise_in_bounds") * high[a]
                total = near + far if total is None else total + (near + far)
            gas_sample = jnp.sum(total * weight_y, axis=0, keepdims=True)
            moving = row(MOVING + c)
            drag = (gas_sample - moving) * rate
            moved_ref[c, pl.ds(k, 1)] = moving + TIME_STEP * drag
            drag_ref[c, pl.ds(k, 1)] = drag

    count = list_ref[0, 2 * room + late]

    @pl.loop(0, (count + UNROLL - 1) // UNROLL)
    def _(group):
        for u in range(UNROLL):
            at = late * room + group * UNROLL + u
            one(list_ref[0, at], list_ref[1, at], list_ref[2, at])


def deposit_kernel(late, size_x, list_ref, table_ref, drag_ref, deposit_in_ref, deposit_ref):
    comps, room = drag_ref.shape[0], (list_ref.shape[1] - 2) // 2
    offsets = offsets_of(comps, size_x)
    packed_z = row_ids(16).astype(jnp.float32).astype(jnp.bfloat16)

    def tall(value):
        return jnp.broadcast_to(value, (16, LANES)).astype(jnp.bfloat16)

    def shares_of(k, first_z):
        def row(i):
            return table_ref[i, pl.ds(k, 1)]

        place = row(IN_Z) + first_z.astype(jnp.float32)
        after = place + 1.0
        after = jnp.where(after == float(LANES), 0.0, after)
        place, after = tall(place), tall(after)
        low_main, low_rest, high_main, high_rest = [tall(row(LOW_MAIN + i)) for i in range(4)]
        nothing = jnp.zeros((16, LANES), jnp.bfloat16)
        main, rest = [], []
        for j in range(LANES // 16):
            here = packed_z + jnp.bfloat16(16 * j)
            at_low, at_high = here == place, here == after
            main.append(jnp.where(at_low, low_main, jnp.where(at_high, high_main, nothing)))
            rest.append(jnp.where(at_low, low_rest, jnp.where(at_high, high_rest, nothing)))
        both = jnp.concatenate(main + rest, axis=0)
        table = jnp.concatenate([both, both], axis=1)
        weight_x = [row(WEIGHT + a) for a in range(REACH_X)]
        weight_y = weight_y_of(table_ref, k)
        pushed = []
        for c in range(comps):
            spread = drag_ref[c, pl.ds(k, 1)] * weight_y
            pushed.extend(spread * weight_x[a] for a in range(REACH_X))
        pushed = jnp.concatenate(pushed, axis=0)
        top = pushed.astype(jnp.bfloat16)
        pushed = jnp.concatenate([top, (pushed - top.astype(jnp.float32)).astype(jnp.bfloat16)], axis=1)
        shares = lax.dot_general(pushed, table, (((1,), (1,)), ((), ())), preferred_element_type=jnp.float32)
        return shares[:, :LANES] + shares[:, LANES:]

    count = list_ref[0, 2 * room + late]

    @pl.loop(0, (count + UNROLL - 1) // UNROLL)
    def _(group):
        at = late * room + group * UNROLL
        shares = [shares_of(list_ref[0, at + u], list_ref[2, at + u]) for u in range(UNROLL)]
        for u in range(UNROLL):
            start = list_ref[1, at + u]
            for i, o in enumerate(offsets):
                spot = pl.ds(start + o, REACH_Y)
                deposit_ref[spot] = deposit_ref[spot] + shares[u][i * REACH_Y : (i + 1) * REACH_Y]


def leave_kernel(crossing_ref, moved_ref, fraction_ref, response_ref, out_ref, velocity_ref):
    comps, nblocks = fraction_ref.shape[:2]
    velocity_ref[...] = moved_ref[:, 0:nblocks]
    for face in range(6):
        for slot in range(crossing_ref.shape[1]):
            block = crossing_ref[face, slot]
            live = block >= 0
            spot = pl.ds(jnp.maximum(block, 0), 1)
            state = [moved_ref[c, spot] for c in range(comps)]
            state = state + [fraction_ref[c, spot] + TIME_STEP * state[c] for c in range(comps)]
            state.append(response_ref[spot])
            for i, value in enumerate(state):
                out_ref[face, i, slot : slot + 1] = jnp.where(live, value, 0.0)


def send_kernel(push, diffuse, size_x, size_y, comps, grid_ref, deposit_ref, leaving_ref, y_ref, x_ref, z_ref):
    rows = leaving_ref.shape[1]
    up = odd("gy")
    y_ref[up, 0:rows] = leaving_ref[2]
    y_ref[1 - up, 0:rows] = leaving_ref[3]
    y_ref[1 - up, rows:] = jnp.zeros((y_ref.shape[1] - rows, LANES), jnp.float32)
    lane = lane_ids(ROWS_Y)
    face = jnp.zeros((ROWS_Y, LANES), jnp.float32)
    for c in range(comps):
        for x in range(size_x + 1):
            at, wrap = row_of(0, c, x, comps, size_x), row_of(1, c, x, comps, size_x)
            beyond = push * deposit_ref[wrap : wrap + ROWS_Y]
            line = slice(at + size_y, at + size_y + 1)
            line = push * deposit_ref[line] + jnp.where(lane_ids(1) == 0, 0.0, beyond[size_y : size_y + 1])
            if x < size_x:
                line = line + diffuse * grid_ref[at + size_y - 1 : at + size_y]
                behind = diffuse * turned(grid_ref[at : at + size_y], 1)
                beyond = jnp.concatenate([beyond[:size_y] + behind, beyond[size_y:]], axis=0)
            else:
                here = grid_ref[at - ROWS_Y : at - ROWS_Y + size_y]
                total = push * deposit_ref[at : at + size_y] + jnp.where(lane_ids(size_y) == 0, 0.0, beyond[:size_y])
                x_ref[c * size_y : (c + 1) * size_y] = diffuse * here + total
            y_ref[up, rows + c * ROWS_Y + x : rows + c * ROWS_Y + x + 1] = line
            place = PACK * c + x
            face = jnp.where(lane == place, turned(beyond, place), face)
    z_ref[...] = face[:size_y]
    y_ref[up, rows + size_x + 1 : rows + size_x + 2] = face[size_y : size_y + 1]


def base_kernel(push, diffuse, grid_ref, deposit_ref, base_ref):
    comps, size_x, size_y, _ = base_ref.shape
    first_lane = lane_ids(size_y) == 0
    for c in range(comps):
        for x in range(size_x):
            at, wrap = row_of(0, c, x, comps, size_x), row_of(1, c, x, comps, size_x)
            here = grid_ref[at : at + size_y]
            laplace = grid_ref[at + ROWS_Y : at + ROWS_Y + size_y]
            if x:
                laplace = laplace + grid_ref[at - ROWS_Y : at - ROWS_Y + size_y]
            laplace = laplace + grid_ref[at + 1 : at + 1 + size_y] + grid_ref[at - 1 : at - 1 + size_y]
            ahead = turned(grid_ref[wrap : wrap + size_y], -1)
            laplace = laplace + ahead + jnp.where(first_lane, 0.0, turned(here, 1)) - 6.0 * here
            total = deposit_ref[at : at + size_y] + jnp.where(first_lane, 0.0, deposit_ref[wrap : wrap + size_y])
            base_ref[c, x] = here + diffuse * laplace + push * total


def below(first_ref, second_ref, rows):
    got = jnp.where(odd("gy") == 1, first_ref[rows], second_ref[rows])
    return jnp.where(lax.axis_index("gy") != 0, got, 0.0)


def relay_kernel(size_x, size_y, comps, count, first_ref, second_ref, x_in_ref, z_in_ref, leaving_ref, x_ref, z_ref, edge_ref):
    edge = comps * size_y
    x_ref[0:edge] = x_in_ref[...]
    for c in range(comps):
        at = count + c * ROWS_Y + size_x
        spot = slice(c * size_y, c * size_y + 1)
        x_ref[spot] = x_in_ref[spot] + below(first_ref, second_ref, slice(at, at + 1))
    x_ref[edge : edge + count] = leaving_ref[0]
    if x_ref.shape[0] > edge + count:
        x_ref[edge + count : edge + 2 * count] = leaving_ref[1]
    at = count + size_x + 1
    edge_ref[...] = z_in_ref[...]
    edge_ref[0:1] = z_in_ref[0:1] + below(first_ref, second_ref, slice(at, at + 1))
    up = odd("gz")
    z_ref[up, 0:count] = leaving_ref[4]
    z_ref[up, count : count + size_y] = edge_ref[...]
    z_ref[1 - up, 0:count] = leaving_ref[5]
    z_ref[1 - up, count : count + size_y] = jnp.zeros((size_y, LANES), jnp.float32)


def finish_kernel(count, base_ref, y1_ref, y2_ref, x_ref, z1_ref, z2_ref, edge_ref, gas_ref):
    comps, size_x, size_y, _ = base_ref.shape
    first_row, first_lane = row_ids(size_y) == 0, lane_ids(size_y) == 0
    rows = slice(count, count + size_y)
    face = jnp.where(odd("gz") == 1, z1_ref[rows], z2_ref[rows])
    corner = edge_ref[...]
    for c in range(comps):
        for x in range(size_x):
            at = count + c * ROWS_Y + x
            line = jnp.broadcast_to(below(y1_ref, y2_ref, slice(at, at + 1)), (size_y, LANES))
            total = base_ref[c, x] + jnp.where(first_row, line, 0.0)
            far = turned(face, -(PACK * c + x))
            if x == 0:
                total = total + x_ref[c * size_y : (c + 1) * size_y]
                far = far + turned(corner, -(PACK * c + size_x))
            gas_ref[c, x] = total + jnp.where(first_lane, far, 0.0)


def per_device(gas_field, velocity, fraction, response, cell_index, brick_index, crossing):
    comps, size_x, size_y, size_z = gas_field.shape
    nblocks = velocity.shape[0]
    loading = 0.5 * size_x * size_y * size_z / (nblocks * 128)
    push, diffuse = -TIME_STEP * loading, TIME_STEP * VISCOSITY
    velocity = jnp.transpose(velocity, (1, 0, 2))
    fraction = jnp.transpose(fraction, (1, 0, 2))
    grid_rows = HEAD + 2 * comps * (size_x + 1) * ROWS_Y
    spare = nblocks + 8

    (face,) = call(pack_face_kernel, [(size_y, LANES)], gas_field)
    plane = gas_field[:, 0].reshape(comps * size_y, LANES)
    from_z = moved_along(face, "gz", -1)
    from_x = moved_along(plane, "gx", -1)
    from_xz = moved_diagonally(face, -1)
    grid, deposit, table, blocks = call(
        prepare_kernel,
        [
            (grid_rows, LANES),
            (grid_rows, LANES),
            (TABLE_ROWS, spare, LANES),
            jax.ShapeDtypeStruct((3, 2 * (nblocks + UNROLL) + 2), jnp.int32),
        ],
        gas_field, velocity, fraction, response, cell_index, brick_index,
        smem=(5,), smem_outs=(3,), cycles=3000,
    )
    line_rows = -(-(comps * size_x + comps + 1) // 8) * 8
    grid, lines = call(
        halo_xz_kernel, [(grid_rows, LANES), (line_rows, LANES)], gas_field, grid, from_z, from_x, from_xz,
        aliases={1: 0},
    )
    y1, y2 = swapped((lines, lines), "gy", False)

    rows_shape = (comps, spare, LANES)
    moved, drag = call(
        functools.partial(drag_kernel, 0, size_x), [rows_shape, rows_shape], blocks, grid, table,
        smem=(0,), cycles=6000,
    )
    deposit = call(
        functools.partial(deposit_kernel, 0, size_x), [(grid_rows, LANES)], blocks, table, drag, deposit,
        smem=(0,), aliases={3: 0}, cycles=6000,
    )[0]
    (grid,) = call(
        functools.partial(halo_y_kernel, comps, size_x, size_y), [(grid_rows, LANES)], grid, y1, y2,
        aliases={0: 0},
    )
    moved, drag = call(
        functools.partial(drag_kernel, 1, size_x), [rows_shape, rows_shape], blocks, grid, table, moved, drag,
        smem=(0,), aliases={3: 0, 4: 1}, cycles=2000,
    )
    deposit = call(
        functools.partial(deposit_kernel, 1, size_x), [(grid_rows, LANES)], blocks, table, drag, deposit,
        smem=(0,), aliases={3: 0}, cycles=2000,
    )[0]

    slots = crossing.shape[1]
    leaving, velocity_next = call(
        leave_kernel, [(6, 7, slots, LANES), (comps, nblocks, LANES)], crossing, moved, fraction, response,
        smem=(0,), cycles=1000,
    )
    count = 7 * slots
    leaving = leaving.reshape(6, count, LANES)
    to_y, to_x, to_z = call(
        functools.partial(send_kernel, push, diffuse, size_x, size_y, comps),
        [(2, count + comps * ROWS_Y, LANES), (comps * size_y, LANES), (size_y, LANES)],
        grid, deposit, leaving, cycles=1000,
    )
    y1, y2 = swapped((to_y[0], to_y[1]), "gy", False)
    (base,) = call(
        functools.partial(base_kernel, push, diffuse), [gas_field.shape], grid, deposit, cycles=2000,
    )
    edge = comps * size_y
    both = lax.axis_size("gx") == 2
    to_x, to_z, to_xz = call(
        functools.partial(relay_kernel, size_x, size_y, comps, count),
        [(edge + (2 if both else 1) * count, LANES), (2, count + size_y, LANES), (size_y, LANES)],
        y1, y2, to_x, to_z, leaving,
    )
    got_x = moved_along(to_x, "gx", 1)
    z1, z2 = swapped((to_z[0], to_z[1]), "gz", True)
    got_xz = moved_diagonally(to_xz, 1)
    got_mx = got_x[edge + count :] if both else moved_along(leaving[1], "gx", -1)
    (gas_next,) = call(
        functools.partial(finish_kernel, count), [gas_field.shape], base, y1, y2, got_x, z1, z2, got_xz,
    )

    j, k = lax.axis_index("gy"), lax.axis_index("gz")
    last = lax.axis_size("gy") - 1
    y1, y2, z1, z2 = y1[:count], y2[:count], z1[:count], z2[:count]
    parts = [
        got_x[edge : edge + count],
        got_mx,
        jnp.where(j == 0, 0.0, jnp.where(j % 2 == 1, y1, y2)),
        jnp.where(j == last, 0.0, jnp.where(j % 2 == 1, y2, y1)),
        jnp.where(k % 2 == 1, z1, z2),
        jnp.where(k % 2 == 1, z2, z1),
    ]
    arrivals = jnp.stack([part.reshape(7, slots, LANES) for part in parts], axis=0)
    return gas_next, jnp.transpose(velocity_next, (1, 0, 2)), jnp.transpose(arrivals, (0, 2, 1, 3))


def solution(mesh):
    owner = ("gx", "gz", "gy")
    in_specs = (
        P(None, "gx", "gy", "gz"),
        P(owner, None, None),
        P(owner, None, None),
        P(owner, None),
        P(owner, None),
        P(owner),
        P(owner, None),
    )
    out_specs = (
        P(None, "gx", "gy", "gz"),
        P(owner, None, None),
        P(owner, None, None, None),
    )
    return jax.shard_map(
        per_device, mesh=mesh, in_specs=in_specs, out_specs=out_specs, check_vma=False
    )
```

time: 44 us -> 47.6 us (1.082)
  the two profiles are of different devices: /device:TPU:0 before, /device:TPU:10 now
where the time goes in v2:
time: 47.6 us; the launch traced here: 47.1 us
  Pallas kernels  20.2 us (42%)
  starting transfers between devices  12.6 us (26%)
  waiting for transfers between devices  7.64 us (16%)
  local copies, waits for them, and re-layouts  5.73 us (12%)
  between operations  0.88 us (2%)
    pallas_call x13, Pallas kernels, call(): pl.pallas_call(body, out_shape=[o if isinstance(o, jax.ShapeDtypeStruct)...  20.2 us
    ppermute x3, starting transfers between devices, swapped(): lax.ppermute(blocks[1], axis, second)  9.3 us
    unnamed x18, local copies, waits for them, and re-layouts  4.97 us
    ppermute x3, starting transfers between devices, moved_along(): lax.ppermute(block, axis, [(i, (i + distance) % count) for i in range(cou...  2.42 us
    ppermute x3, waiting for transfers between devices, swapped(): lax.ppermute(blocks[1], axis, second)  2.34 us
    ppermute x2, waiting for transfers between devices, moved_diagonally(): return lax.ppermute(block, ('gx', 'gz'), route)  2.17 us
    ppermute x3, waiting for transfers between devices, swapped(): lax.ppermute(blocks[0], axis, first)  1.99 us
    ppermute x3, waiting for transfers between devices, moved_along(): lax.ppermute(block, axis, [(i, (i + distance) % count) for i in range(cou...  1.15 us
  transfers between devices with their start and end apart: 11, of which 5 were waited for; matrix products, arithmetic and copies ran while one was open for 0% of the time, Pallas kernels for 24%

profile of v2, /device:TPU:10, one launch (start us, length us, event | category | flops | bytes accessed | tf_op | source)
XLA Modules:
  0.0 47.1 jit_solution(12133742547962378721)
XLA Ops:
  0.6 0.7 %slice.33 = f32[3,1,16,128]{3,2,1,0:T(8,128)S(1)} slice(f32[3,16,16,128]{3,2,1,0:T(8,128)} %gas_ref.5), slice={[0:3], [0:1], [0:16], [0:128]} | slice | bytes 49152 | tf_op jit(solution)/shard_map/slice | solution.py:426
  1.4 1.5 %collective-permute-start.1 = (f32[48,128]{1,0:T(8,128)S(1)}, f32[48,128]{1,0:T(8,128)S(1)}, u32[]{:S(2)}, u32[]{:S(2)}) collective-permute-start(f32[48,128]{1,0:T(8,128)S(1)} %bitcast.35), channel_id=1, source_target_pairs={{0,16},{16,0},{1,17},{17,1},{2,18},{18,2},{3,19},{19,3},{4,20},{20... | collective-permute-start | bytes 73736 | tf_op jit(solution)/shard_map/ppermute | solution.py:35
  2.9 0.0 copy-start
  2.9 1.0 %copy-done = f32[3,16,16,128]{3,2,1,0:T(8,128)S(1)} copy-done((f32[3,16,16,128]{3,2,1,0:T(8,128)S(1)}, f32[3,16,16,128]{3,2,1,0:T(8,128)}, u32[]{:S(2)}) %copy-start) | copy-done | bytes 393240
  3.9 0.2 shard_map.95
  4.1 0.1 collective-permute-start
  4.1 0.6 %collective-permute-start.2 = (f32[16,128]{1,0:T(8,128)S(1)}, f32[16,128]{1,0:T(8,128)S(1)}, u32[]{:S(2)}, u32[]{:S(2)}) collective-permute-start(f32[16,128]{1,0:T(8,128)S(1)} %shard_map.95), channel_id=1, source_target_pairs={{0,28},{4,16},{8,20},{12,24},{16,12},{20,0},{24,4},{28,8},{1,29},{... | collective-permute-start | bytes 24584 | tf_op jit(solution)/shard_map/ppermute | solution.py:50
  4.7 0.0 copy-start.1
  4.7 0.9 %copy-done.1 = f32[64,3,128]{2,0,1:T(8,128)S(1)} copy-done((f32[64,3,128]{2,0,1:T(8,128)S(1)}, f32[64,3,128]{2,0,1:T(8,128)}, u32[]{:S(2)}) %copy-start.1) | copy-done | bytes 98328
  5.6 0.0 copy-start.2
  5.6 0.8 %copy-done.2 = f32[64,128]{1,0:T(8,128)S(1)} copy-done((f32[64,128]{1,0:T(8,128)S(1)}, f32[64,128]{1,0:T(8,128)}, u32[]{:S(2)}) %copy-start.2) | copy-done | bytes 32792
  6.4 0.9 %copy-done.3 = f32[64,3,128]{2,0,1:T(8,128)S(1)} copy-done((f32[64,3,128]{2,0,1:T(8,128)S(1)}, f32[64,3,128]{2,0,1:T(8,128)}, u32[]{:S(2)}) %copy-start.3) | copy-done | bytes 98328
  7.2 0.8 %copy-done.4 = s32[64,128]{1,0:T(8,128)S(1)} copy-done((s32[64,128]{1,0:T(8,128)S(1)}, s32[64,128]{1,0:T(8,128)}, u32[]{:S(2)}) %copy-start.4) | copy-done | bytes 32792
  8.0 0.7 %copy-done.6 = s32[64]{0:T(128)S(1)} copy-done((s32[64]{0:T(128)S(1)}, s32[64]{0:T(128)}, u32[]{:S(2)}) %copy-start.6) | copy-done | bytes 280
  8.7 3.2 %shard_map.94 = (f32[2456,128]{1,0:T(8,128)S(1)}, f32[2456,128]{1,0:T(8,128)S(1)}, f32[26,72,128]{2,1,0:T(8,128)S(1)}, s32[3,146]{1,0:T(4,128)S(1)}) custom-call(f32[3,16,16,128]{3,2,1,0:T(8,128)S(1)} %copy-done, f32[3,64,128]{2,1,0:T(8,128)S(1)} %bitcast.34, f32[3,64,128]{2,1,0:T(8,128)S(1)} %bitcast.32, f32[64,128]{1,0:T(8,128)S(1)} %copy-done.2, ...), custom_call_target="tpu_custom_call" | custom-call | flops 12288000 | bytes 3072000 | tf_op jit(solution)/shard_map/pallas_call | solution.py:54
  11.9 0.0 collective-permute-done.face_ref
  11.9 0.0 collective-permute-done.2.edge_ref
  11.9 0.0 collective-permute-done.1.from_x_ref
  11.9 0.2 shard_map.96
  12.1 0.1 collective-permute-start.3
  12.1 5.0 %collective-permute-start.4 = (f32[56,128]{1,0:T(8,128)S(1)}, f32[56,128]{1,0:T(8,128)S(1)}, u32[]{:S(2)}, u32[]{:S(2)}) collective-permute-start(f32[56,128]{1,0:T(8,128)S(1)} %get-tuple-element.23), channel_id=1, source_target_pairs={{0,0},{1,2},{2,1},{3,3},{4,4},{5,6},{6,5},{7,7},{8,8},{9,10},{10,9... | collective-permute-start | bytes 86024 | tf_op jit(solution)/shard_map/ppermute | solution.py:44
  17.2 4.0 %shard_map.98 = (f32[3,72,128]{2,1,0:T(8,128)S(1)}, f32[3,72,128]{2,1,0:T(8,128)S(1)}) custom-call(s32[3,146]{1,0:T(4,128)S(1)} %get-tuple-element.24.list_ref, f32[2456,128]{1,0:T(8,128)S(1)} %get-tuple-element.22.grid_in_ref.grid_ref, f32[26,72,128]{2,1,0:T(8,128)S(1)} %get-tuple-element.25.table_ref), custom_call_target="tpu_custom_call" | custom-call | flops 24576000 | bytes 6144000 | tf_op jit(solution)/shard_map/pallas_call | solution.py:54
  21.2 3.6 %shard_map.100.deposit_in_ref = f32[2456,128]{1,0:T(8,128)S(1)} custom-call(s32[3,146]{1,0:T(4,128)S(1)} %get-tuple-element.24.list_ref, f32[26,72,128]{2,1,0:T(8,128)S(1)} %get-tuple-element.25.table_ref, f32[3,72,128]{2,1,0:T(8,128)S(1)} %get-tuple-element.27.refs_1_.drag_ref, ...), custom_call_target="tpu_custom_call", output_to_operand_aliasing={{}: (3, {})} | custom-call | flops 24576000 | bytes 6144000 | tf_op jit(solution)/shard_map/pallas_call | solution.py:54
  24.9 0.0 collective-permute-done.3.first_ref
  24.9 0.0 collective-permute-done.4.second_ref
  24.9 0.1 shard_map.97.grid_ref
  25.0 2.3 %shard_map.99 = (f32[3,72,128]{2,1,0:T(8,128)S(1)}, f32[3,72,128]{2,1,0:T(8,128)S(1)}) custom-call(s32[3,146]{1,0:T(4,128)S(1)} %get-tuple-element.24.list_ref, f32[2456,128]{1,0:T(8,128)S(1)} %shard_map.97.grid_ref, f32[26,72,128]{2,1,0:T(8,128)S(1)} %get-tuple-element.25.table_ref, ...), custom_call_target="tpu_custom_call", output_to_operand_aliasing={{0}: (3, {}), {1}: (4, {})} | custom-call | flops 8192000 | bytes 2048000 | tf_op jit(solution)/shard_map/pallas_call | solution.py:54
  27.3 0.0 copy-start.5
  27.4 2.1 %shard_map.101.deposit_ref = f32[2456,128]{1,0:T(8,128)S(1)} custom-call(s32[3,146]{1,0:T(4,128)S(1)} %get-tuple-element.24.list_ref, f32[26,72,128]{2,1,0:T(8,128)S(1)} %get-tuple-element.25.table_ref, f32[3,72,128]{2,1,0:T(8,128)S(1)} %get-tuple-element.28.drag_ref, f32[2456,128]{1,0:T(8,128)S(1)} %shard_map.100.deposit_in_ref), custom_call_target="tpu_custom_call", output_to_operand_aliasing={{}: (3, {})} | custom-call | flops 8192000 | bytes 2048000 | tf_op jit(solution)/shard_map/pallas_call | solution.py:54
  29.5 0.0 copy-done.5
  29.5 1.4 %shard_map.103 = (f32[6,7,8,128]{3,2,1,0:T(8,128)S(1)}, f32[3,64,128]{2,1,0:T(8,128)}) custom-call(s32[6,8]{1,0:T(8,128)S(1)} %copy-done.5, f32[3,72,128]{2,1,0:T(8,128)S(1)} %get-tuple-element.30.moved_ref, f32[3,64,128]{2,1,0:T(8,128)S(1)} %bitcast.33, f32[64,128]{1,0:T(8,128)S(1)} %copy-done.2), custom_call_target="tpu_custom_call" | custom-call | flops 4096000 | bytes 1024000 | tf_op jit(solution)/shard_map/pallas_call | solution.py:54
  31.0 1.7 %shard_map.104 = (f32[2,128,128]{2,1,0:T(8,128)S(1)}, f32[48,128]{1,0:T(8,128)S(1)}, f32[16,128]{1,0:T(8,128)S(1)}) custom-call(f32[2456,128]{1,0:T(8,128)S(1)} %shard_map.97.grid_ref, f32[2456,128]{1,0:T(8,128)S(1)} %shard_map.101.deposit_ref, f32[6,56,128]{2,1,0:T(8,128)S(1)} %bitcast.30), custom_call_target="tpu_custom_call" | custom-call | flops 4096000 | bytes 1024000 | tf_op jit(solution)/shard_map/pallas_call | solution.py:54
  32.7 0.1 collective-permute-start.5
  32.8 1.9 %collective-permute-start.6 = (f32[128,128]{1,0:T(8,128)S(1)}, f32[128,128]{1,0:T(8,128)S(1)}, u32[]{:S(2)}, u32[]{:S(2)}) collective-permute-start(f32[128,128]{1,0:T(8,128)S(1)} %get-tuple-element.39), channel_id=1, source_target_pairs={{0,0},{1,2},{2,1},{3,3},{4,4},{5,6},{6,5},{7,7},{8,8},{9,10},{10,9... | collective-permute-start | bytes 196616 | tf_op jit(solution)/shard_map/ppermute | solution.py:44
  34.8 0.3 shard_map.102.base_ref
  35.1 2.0 %collective-permute-done.5.first_ref.y1_ref = f32[128,128]{1,0:T(8,128)S(1)} collective-permute-done((f32[128,128]{1,0:T(8,128)S(1)}, f32[128,128]{1,0:T(8,128)S(1)}, u32[]{:S(2)}, u32[]{:S(2)}) %collective-permute-start.5) | collective-permute-done | bytes 65568 | tf_op jit(solution)/shard_map/ppermute | solution.py:44
  37.1 1.9 %collective-permute-done.6.second_ref.y2_ref = f32[128,128]{1,0:T(8,128)S(1)} collective-permute-done((f32[128,128]{1,0:T(8,128)S(1)}, f32[128,128]{1,0:T(8,128)S(1)}, u32[]{:S(2)}, u32[]{:S(2)}) %collective-permute-start.6) | collective-permute-done | bytes 65568 | tf_op jit(solution)/shard_map/ppermute | solution.py:44
  39.0 0.8 %collective-permute-start.7 = (f32[160,128]{1,0:T(8,128)S(1)}, f32[160,128]{1,0:T(8,128)S(1)}, u32[]{:S(2)}, u32[]{:S(2)}) collective-permute-start(f32[160,128]{1,0:T(8,128)S(1)} %get-tuple-element.35), channel_id=1, source_target_pairs={{0,16},{16,0},{1,17},{17,1},{2,18},{18,2},{3,19},{19,3},{4,20},{20... | collective-permute-start | bytes 245768 | tf_op jit(solution)/shard_map/ppermute | solution.py:35
  39.9 0.0 collective-permute-start.8
  39.9 2.3 %collective-permute-start.9 = (f32[72,128]{1,0:T(8,128)S(1)}, f32[72,128]{1,0:T(8,128)S(1)}, u32[]{:S(2)}, u32[]{:S(2)}) collective-permute-start(f32[72,128]{1,0:T(8,128)S(1)} %get-tuple-element.41), channel_id=1, source_target_pairs={{0,12},{4,8},{8,4},{12,0},{1,13},{5,9},{9,5},{13,1},{2,14},{6,10},... | collective-permute-start | bytes 110600 | tf_op jit(solution)/shard_map/ppermute | solution.py:44
  42.2 0.2 collective-permute-start.10
  42.4 1.1 %collective-permute-done.7.x_ref = f32[160,128]{1,0:T(8,128)S(1)} collective-permute-done((f32[160,128]{1,0:T(8,128)S(1)}, f32[160,128]{1,0:T(8,128)S(1)}, u32[]{:S(2)}, u32[]{:S(2)}) %collective-permute-start.7) | collective-permute-done | bytes 81952 | tf_op jit(solution)/shard_map/ppermute | solution.py:35
  43.5 0.0 collective-permute-done.8.z1_ref
  43.6 0.4 collective-permute-done.9.z2_ref
  44.0 0.0 copy-start.7
  44.0 2.2 %collective-permute-done.10.edge_ref = f32[16,128]{1,0:T(8,128)S(1)} collective-permute-done((f32[16,128]{1,0:T(8,128)S(1)}, f32[16,128]{1,0:T(8,128)S(1)}, u32[]{:S(2)}, u32[]{:S(2)}) %collective-permute-start.10) | collective-permute-done | bytes 8224 | tf_op jit(solution)/shard_map/ppermute | solution.py:50
  46.2 0.9 %shard_map.106 = f32[3,16,16,128]{3,2,1,0:T(8,128)} custom-call(f32[3,16,16,128]{3,2,1,0:T(8,128)S(1)} %shard_map.102.base_ref, f32[128,128]{1,0:T(8,128)S(1)} %collective-permute-done.5.first_ref.y1_ref, f32[128,128]{1,0:T(8,128)S(1)} %collective-permute-done.6.second_ref.y2_ref, f32[160,128]{1,0:T(8,128)S(1)} %collective-permute-done.7.x_ref, ...), custom_call_target="tpu_custom_call" | custom-call | tf_op jit(solution)/shard_map/pallas_call | solution.py:54
  47.1 0.0 copy-done.7
  (12 shorter events, 0.1 us)
Async XLA Ops:
  1.4 10.5 %collective-permute-start.1 = (f32[48,128]{1,0:T(8,128)S(1)}, f32[48,128]{1,0:T(8,128)S(1)}, u32[]{:S(2)}, u32[]{:S(2)}) collective-permute-start(f32[48,128]{1,0:T(8,128)S(1)} %bitcast.35), channel_id=1, source_target_pairs={{0,16},{16,0},{1,17},{17,1},{2,18},{18,2},{3,19},{19,3},{4,20},{20... | collective-permute-start | bytes 73736 | tf_op jit(solution)/shard_map/ppermute | solution.py:35
  2.9 1.0 %copy-start = (f32[3,16,16,128]{3,2,1,0:T(8,128)S(1)}, f32[3,16,16,128]{3,2,1,0:T(8,128)}, u32[]{:S(2)}) copy-start(f32[3,16,16,128]{3,2,1,0:T(8,128)} %gas_ref.5) | copy-start | bytes 1179652
  4.1 7.8 %collective-permute-start = (f32[16,128]{1,0:T(8,128)S(1)}, f32[16,128]{1,0:T(8,128)S(1)}, u32[]{:S(2)}, u32[]{:S(2)}) collective-permute-start(f32[16,128]{1,0:T(8,128)S(1)} %shard_map.95), channel_id=1, source_target_pairs={{0,12},{4,0},{8,4},{12,8},{1,13},{5,1},{9,5},{13,9},{2,14},{6,2},{... | collective-permute-start | bytes 24584 | tf_op jit(solution)/shard_map/ppermute | solution.py:35
  4.1 7.8 %collective-permute-start.2 = (f32[16,128]{1,0:T(8,128)S(1)}, f32[16,128]{1,0:T(8,128)S(1)}, u32[]{:S(2)}, u32[]{:S(2)}) collective-permute-start(f32[16,128]{1,0:T(8,128)S(1)} %shard_map.95), channel_id=1, source_target_pairs={{0,28},{4,16},{8,20},{12,24},{16,12},{20,0},{24,4},{28,8},{1,29},{... | collective-permute-start | bytes 24584 | tf_op jit(solution)/shard_map/ppermute | solution.py:50
  4.7 0.9 %copy-start.1 = (f32[64,3,128]{2,0,1:T(8,128)S(1)}, f32[64,3,128]{2,0,1:T(8,128)}, u32[]{:S(2)}) copy-start(f32[64,3,128]{2,0,1:T(8,128)} %param.9) | copy-start | bytes 294916
  5.6 0.8 %copy-start.2 = (f32[64,128]{1,0:T(8,128)S(1)}, f32[64,128]{1,0:T(8,128)}, u32[]{:S(2)}) copy-start(f32[64,128]{1,0:T(8,128)} %response_ref.3) | copy-start | bytes 98308
  6.3 0.9 %copy-start.3 = (f32[64,3,128]{2,0,1:T(8,128)S(1)}, f32[64,3,128]{2,0,1:T(8,128)}, u32[]{:S(2)}) copy-start(f32[64,3,128]{2,0,1:T(8,128)} %param.8) | copy-start | bytes 294916
  7.2 0.8 %copy-start.4 = (s32[64,128]{1,0:T(8,128)S(1)}, s32[64,128]{1,0:T(8,128)}, u32[]{:S(2)}) copy-start(s32[64,128]{1,0:T(8,128)} %cell_ref.1) | copy-start | bytes 98308
  8.0 0.7 %copy-start.6 = (s32[64]{0:T(128)S(1)}, s32[64]{0:T(128)}, u32[]{:S(2)}) copy-start(s32[64]{0:T(128)} %brick_ref.1) | copy-start | bytes 772
  12.1 12.8 %collective-permute-start.3 = (f32[56,128]{1,0:T(8,128)S(1)}, f32[56,128]{1,0:T(8,128)S(1)}, u32[]{:S(2)}, u32[]{:S(2)}) collective-permute-start(f32[56,128]{1,0:T(8,128)S(1)} %get-tuple-element.23), channel_id=1, source_target_pairs={{0,1},{1,0},{2,3},{3,2},{4,5},{5,4},{6,7},{7,6},{8,9},{9,8},{10,11... | collective-permute-start | bytes 86024 | tf_op jit(solution)/shard_map/ppermute | solution.py:44
  12.1 12.7 %collective-permute-start.4 = (f32[56,128]{1,0:T(8,128)S(1)}, f32[56,128]{1,0:T(8,128)S(1)}, u32[]{:S(2)}, u32[]{:S(2)}) collective-permute-start(f32[56,128]{1,0:T(8,128)S(1)} %get-tuple-element.23), channel_id=1, source_target_pairs={{0,0},{1,2},{2,1},{3,3},{4,4},{5,6},{6,5},{7,7},{8,8},{9,10},{10,9... | collective-permute-start | bytes 86024 | tf_op jit(solution)/shard_map/ppermute | solution.py:44
  27.3 2.2 %copy-start.5 = (s32[6,8]{1,0:T(8,128)S(1)}, s32[6,8]{1,0:T(8,128)}, u32[]{:S(2)}) copy-start(s32[6,8]{1,0:T(8,128)} %crossing_ref.1) | copy-start | bytes 580
  32.7 4.3 %collective-permute-start.5 = (f32[128,128]{1,0:T(8,128)S(1)}, f32[128,128]{1,0:T(8,128)S(1)}, u32[]{:S(2)}, u32[]{:S(2)}) collective-permute-start(f32[128,128]{1,0:T(8,128)S(1)} %get-tuple-element.40), channel_id=1, source_target_pairs={{0,1},{1,0},{2,3},{3,2},{4,5},{5,4},{6,7},{7,6},{8,9},{9,8},{10,11... | collective-permute-start | bytes 196616 | tf_op jit(solution)/shard_map/ppermute | solution.py:44
  32.8 6.2 %collective-permute-start.6 = (f32[128,128]{1,0:T(8,128)S(1)}, f32[128,128]{1,0:T(8,128)S(1)}, u32[]{:S(2)}, u32[]{:S(2)}) collective-permute-start(f32[128,128]{1,0:T(8,128)S(1)} %get-tuple-element.39), channel_id=1, source_target_pairs={{0,0},{1,2},{2,1},{3,3},{4,4},{5,6},{6,5},{7,7},{8,8},{9,10},{10,9... | collective-permute-start | bytes 196616 | tf_op jit(solution)/shard_map/ppermute | solution.py:44
  39.0 4.5 %collective-permute-start.7 = (f32[160,128]{1,0:T(8,128)S(1)}, f32[160,128]{1,0:T(8,128)S(1)}, u32[]{:S(2)}, u32[]{:S(2)}) collective-permute-start(f32[160,128]{1,0:T(8,128)S(1)} %get-tuple-element.35), channel_id=1, source_target_pairs={{0,16},{16,0},{1,17},{17,1},{2,18},{18,2},{3,19},{19,3},{4,20},{20... | collective-permute-start | bytes 245768 | tf_op jit(solution)/shard_map/ppermute | solution.py:35
  39.9 3.7 %collective-permute-start.8 = (f32[72,128]{1,0:T(8,128)S(1)}, f32[72,128]{1,0:T(8,128)S(1)}, u32[]{:S(2)}, u32[]{:S(2)}) collective-permute-start(f32[72,128]{1,0:T(8,128)S(1)} %get-tuple-element.42), channel_id=1, source_target_pairs={{0,4},{4,0},{8,12},{12,8},{1,5},{5,1},{9,13},{13,9},{2,6},{6,2},{1... | collective-permute-start | bytes 110600 | tf_op jit(solution)/shard_map/ppermute | solution.py:44
  39.9 4.1 %collective-permute-start.9 = (f32[72,128]{1,0:T(8,128)S(1)}, f32[72,128]{1,0:T(8,128)S(1)}, u32[]{:S(2)}, u32[]{:S(2)}) collective-permute-start(f32[72,128]{1,0:T(8,128)S(1)} %get-tuple-element.41), channel_id=1, source_target_pairs={{0,12},{4,8},{8,4},{12,0},{1,13},{5,9},{9,5},{13,1},{2,14},{6,10},... | collective-permute-start | bytes 110600 | tf_op jit(solution)/shard_map/ppermute | solution.py:44
  42.2 4.0 %collective-permute-start.10 = (f32[16,128]{1,0:T(8,128)S(1)}, f32[16,128]{1,0:T(8,128)S(1)}, u32[]{:S(2)}, u32[]{:S(2)}) collective-permute-start(f32[16,128]{1,0:T(8,128)S(1)} %get-tuple-element.37), channel_id=1, source_target_pairs={{0,20},{4,24},{8,28},{12,16},{16,4},{20,8},{24,12},{28,0},{1,21},{... | collective-permute-start | bytes 24584 | tf_op jit(solution)/shard_map/ppermute | solution.py:50
  44.0 3.1 %copy-start.7 = (f32[6,7,8,128]{3,2,1,0:T(8,128)}, f32[6,7,8,128]{3,2,1,0:T(8,128)S(1)}, u32[]{:S(2)}) copy-start(f32[6,7,8,128]{3,2,1,0:T(8,128)S(1)} %bitcast_dynamic-update-slice_fusion) | copy-start | bytes 516100
